TPU v7x, 128 devices: a whole 4x4x4 slice. The times are simulated.
128 devices in a mesh: lon: 16 (over y, x_lo, core), lat: 8 (over z, x_hi).
Axes of the slice: x: 4 (x_hi: 2, x_lo: 2; x = x_hi * 2 + x_lo), y: 4, z: 4, core: 2. Of those that a mesh axis runs over, the one named last changes fastest.
Arguments:
- tokens: bfloat16 [4, 384, 48, 512], P(None, 'lon', 'lat'), may hold values from -6 to 6
- cotangent: bfloat16 [4, 192, 24, 1024], P(None, 'lon', 'lat'), may hold values from -6 to 6
- fine_qkv: bfloat16 [512, 1536], replicated, may hold values from -3 to 3
- fine_out: bfloat16 [512, 512], replicated, may hold values from -0.25 to 0.25
- merge_weight: bfloat16 [2048, 1024], replicated, may hold values from -0.125 to 0.125
- coarse_qkv: bfloat16 [1024, 3072], replicated, may hold values from -3 to 3
- coarse_out: bfloat16 [1024, 1024], replicated, may hold values from -0.1875 to 0.1875
Outputs:
- coarse: bfloat16 [4, 192, 24, 1024], P(None, 'lon', 'lat')
- d_tokens: bfloat16 [4, 384, 48, 512], P(None, 'lon', 'lat')
- grad_fine_qkv: float32 [512, 1536], P(('lon', 'lat'))
- grad_fine_out: float32 [512, 512], P(('lon', 'lat'))
- grad_merge: float32 [2048, 1024], P(('lon', 'lat'))
- grad_coarse_qkv: float32 [1024, 3072], P(('lon', 'lat'))
- grad_coarse_out: float32 [1024, 1024], P(('lon', 'lat'))
All inputs are finite; a program needn't handle non-finite values.
Results may differ from a plain program's by a relative error of at most 0.03.
Values may be sent and summed in bfloat16 or wider, within the bound.
No kernel may reach another device: no remote copies, remote signals or barrier semaphores. Data moves between devices by JAX's collectives and lax.ppermute only.
A program may use at most 128 MiB of HBM per device.

v0:
```python
import jax
import jax.numpy as jnp
from jax import lax
from jax.sharding import PartitionSpec as P

HEADS = 8
HEADS2 = 16
WIN_LEV = 2
WIN_LON = 12
WIN_LAT = 6
SHIFT = 6


NORM_EPS = 1e-05


def passed_along(block, axis, distance):
    devices = range(lax.axis_size(axis))
    route = [((i - distance) % len(devices), i) for i in devices]
    return lax.ppermute(block, axis, route)


def from_partner(block, axis, distance):
    count = lax.axis_size(axis)
    route = []
    for low in range(count):
        high = low | 1 << distance
        if high != low and high < count:
            route += [(low, high), (high, low)]
    return lax.ppermute(block, axis, route)


def to_half(tensor):
    return tensor.astype(jnp.bfloat16)


def layer_norm(vector_in):
    mean_val = jnp.mean(vector_in, axis=-1, keepdims=True)
    centred = vector_in - mean_val
    variance = jnp.mean(centred * centred, axis=-1, keepdims=True)
    return centred * lax.rsqrt(variance + NORM_EPS)


def norm_back(vector_in, upstream):
    return jax.vjp(layer_norm, vector_in)[1](upstream)[0]


def to_windows(grid_vals, lon_span, lat_span):
    levels, columns, latitudes, channels = grid_vals.shape
    blocks = grid_vals.reshape(
        levels // WIN_LEV,
        WIN_LEV,
        columns // lon_span,
        lon_span,
        latitudes // lat_span,
        lat_span,
        channels,
    )
    blocks = blocks.transpose(0, 2, 4, 1, 3, 5, 6)
    return blocks.reshape(-1, WIN_LEV * lon_span * lat_span, channels)


def from_windows(windows, levels, columns, latitudes, lon_span, lat_span):
    channels = windows.shape[-1]
    blocks = windows.reshape(
        levels // WIN_LEV,
        columns // lon_span,
        latitudes // lat_span,
        WIN_LEV,
        lon_span,
        lat_span,
        channels,
    )
    return blocks.transpose(0, 3, 1, 4, 2, 5, 6).reshape(levels, columns, latitudes, channels)


def split_heads(tensor, heads):
    return tensor.reshape(tensor.shape[0], tensor.shape[1], heads, tensor.shape[2] // heads)


def attend(queries, key_rows, value_rows, heads):
    scores = jnp.einsum(
        "bqhd,bkhd->bhqk",
        split_heads(queries, heads),
        split_heads(key_rows, heads),
        preferred_element_type=jnp.float32,
    )
    attn_probs = jax.nn.softmax(scores, axis=-1)
    attn_weights = to_half(attn_probs)
    context = jnp.einsum(
        "bhqk,bkhd->bqhd",
        attn_weights,
        split_heads(value_rows, heads),
        preferred_element_type=jnp.float32,
    )
    return (to_half(context.reshape(queries.shape)), attn_probs, attn_weights)


def attend_back(queries, key_rows, value_rows, attn_probs, attn_weights, d_context, heads):
    query_heads = split_heads(queries, heads)
    key_heads = split_heads(key_rows, heads)
    d_ctx_heads = split_heads(d_context, heads)
    d_weights = jnp.einsum(
        "bqhd,bkhd->bhqk",
        d_ctx_heads,
        split_heads(value_rows, heads),
        preferred_element_type=jnp.float32,
    )
    d_values = jnp.einsum(
        "bhqk,bqhd->bkhd", attn_weights, d_ctx_heads, preferred_element_type=jnp.float32
    )
    d_scores = attn_probs * (d_weights - jnp.sum(d_weights * attn_probs, axis=-1, keepdims=True))
    d_half = to_half(d_scores)
    d_queries = jnp.einsum("bhqk,bkhd->bqhd", d_half, key_heads, preferred_element_type=jnp.float32)
    d_keys = jnp.einsum("bhqk,bqhd->bkhd", d_half, query_heads, preferred_element_type=jnp.float32)
    return (
        d_queries.reshape(queries.shape),
        d_keys.reshape(key_rows.shape),
        d_values.reshape(value_rows.shape),
    )


def block_forward(windows, w_qkv, w_out, heads):
    channels = windows.shape[-1]
    query_scale = (channels // heads) ** (-0.5)
    normed = to_half(layer_norm(windows.astype(jnp.float32)))
    qkv = jnp.dot(normed, w_qkv, preferred_element_type=jnp.float32)
    queries = to_half(qkv[..., :channels] * query_scale)
    key_rows = to_half(qkv[..., channels : 2 * channels])
    value_rows = to_half(qkv[..., 2 * channels :])
    context, attn_probs, attn_weights = attend(queries, key_rows, value_rows, heads)
    projected = jnp.dot(context, w_out, preferred_element_type=jnp.float32)
    result = to_half(windows.astype(jnp.float32) + projected)
    return (result, (normed, queries, key_rows, value_rows, attn_probs, attn_weights, context))


def block_backward(windows, stash, d_result, w_qkv, w_out, heads):
    normed, queries, key_rows, value_rows, attn_probs, attn_weights, context = stash
    channels = windows.shape[-1]
    query_scale = (channels // heads) ** (-0.5)
    grad_out = jnp.dot(
        context.reshape(-1, channels).T,
        d_result.reshape(-1, channels),
        preferred_element_type=jnp.float32,
    )
    d_context = to_half(jnp.dot(d_result, w_out.T, preferred_element_type=jnp.float32))
    d_queries, d_keys, d_values = attend_back(
        queries, key_rows, value_rows, attn_probs, attn_weights, d_context, heads
    )
    d_qkv = to_half(jnp.concatenate([d_queries * query_scale, d_keys, d_values], axis=-1))
    grad_qkv = jnp.dot(
        normed.reshape(-1, channels).T,
        d_qkv.reshape(-1, 3 * channels),
        preferred_element_type=jnp.float32,
    )
    d_normed = jnp.dot(d_qkv, w_qkv.T, preferred_element_type=jnp.float32)
    d_normed = lax.optimization_barrier(to_half(d_normed))
    d_windows = to_half(
        d_result.astype(jnp.float32)
        + norm_back(windows.astype(jnp.float32), d_normed.astype(jnp.float32))
    )
    return (d_windows, grad_qkv, grad_out)


def merge_forward(fine_grid, w_merge):
    levels, columns, latitudes, channels = fine_grid.shape
    stacked = fine_grid.reshape(levels, columns // 2, 2, latitudes // 2, 2, channels)
    stacked = stacked.transpose(0, 1, 3, 2, 4, 5).reshape(
        levels, columns // 2, latitudes // 2, 4 * channels
    )
    normed = to_half(layer_norm(stacked.astype(jnp.float32)))
    merged = to_half(jnp.dot(normed, w_merge, preferred_element_type=jnp.float32))
    return (merged, stacked, normed)


def merge_backward(stacked, normed, d_merged, w_merge, channels):
    wide_channels = d_merged.shape[-1]
    grad_merge = jnp.dot(
        normed.reshape(-1, 4 * channels).T,
        d_merged.reshape(-1, wide_channels),
        preferred_element_type=jnp.float32,
    )
    d_normed = lax.optimization_barrier(
        to_half(jnp.dot(d_merged, w_merge.T, preferred_element_type=jnp.float32))
    )
    d_stacked = to_half(norm_back(stacked.astype(jnp.float32), d_normed.astype(jnp.float32)))
    levels = d_stacked.shape[0]
    half_cols = d_stacked.shape[1]
    half_lats = d_stacked.shape[2]
    d_fine = d_stacked.reshape(levels, half_cols, half_lats, 2, 2, channels).transpose(
        0, 1, 3, 2, 4, 5
    )
    return (d_fine.reshape(levels, 2 * half_cols, 2 * half_lats, channels), grad_merge)


def local(tokens, cotangent, fine_qkv, fine_out, merge_weight, coarse_qkv, coarse_out):
    levels, columns, latitudes, channels = tokens.shape
    incoming = passed_along(tokens[:, :SHIFT], "lon", -1)
    shifted = jnp.concatenate([tokens[:, SHIFT:], incoming], axis=1)
    fine_windows = to_windows(shifted, WIN_LON, WIN_LAT)
    fine_results, fine_stash = block_forward(fine_windows, fine_qkv, fine_out, HEADS)
    fine_shifted_out = from_windows(fine_results, levels, columns, latitudes, WIN_LON, WIN_LAT)
    tail_cols = passed_along(fine_shifted_out[:, columns - SHIFT :], "lon", 1)
    fine_state = jnp.concatenate([tail_cols, fine_shifted_out[:, : columns - SHIFT]], axis=1)
    merged, stacked, merge_normed = merge_forward(fine_state, merge_weight)
    wide_channels = merged.shape[-1]
    half_lat = latitudes // 2
    coarse_scale = (wide_channels // HEADS2) ** (-0.5)
    own_windows = to_windows(merged, WIN_LON, half_lat)
    coarse_normed = to_half(layer_norm(own_windows.astype(jnp.float32)))
    coarse_proj = jnp.dot(coarse_normed, coarse_qkv, preferred_element_type=jnp.float32)
    queries = to_half(coarse_proj[..., :wide_channels] * coarse_scale)
    near_keys = to_half(coarse_proj[..., wide_channels : 2 * wide_channels])
    near_values = to_half(coarse_proj[..., 2 * wide_channels :])
    far_keys, far_values = from_partner((near_keys, near_values), "lat", 0)
    key_rows = jnp.concatenate([near_keys, far_keys], axis=1)
    value_rows = jnp.concatenate([near_values, far_values], axis=1)
    context, attn_probs, attn_weights = attend(queries, key_rows, value_rows, HEADS2)
    projected = jnp.dot(context, coarse_out, preferred_element_type=jnp.float32)
    coarse_res = to_half(own_windows.astype(jnp.float32) + projected)
    coarse = from_windows(coarse_res, levels, columns // 2, half_lat, WIN_LON, half_lat)
    cot_windows = to_windows(cotangent, WIN_LON, half_lat)
    grad_cout = jnp.dot(
        context.reshape(-1, wide_channels).T,
        cot_windows.reshape(-1, wide_channels),
        preferred_element_type=jnp.float32,
    )
    d_context = to_half(jnp.dot(cot_windows, coarse_out.T, preferred_element_type=jnp.float32))
    d_queries, d_keys, d_values = attend_back(
        queries, key_rows, value_rows, attn_probs, attn_weights, d_context, HEADS2
    )
    half_len = own_windows.shape[1]
    back_keys, back_values = (
        from_partner(d_keys[:, half_len:].astype(jnp.bfloat16), "lat", 0).astype(jnp.float32),
        from_partner(d_values[:, half_len:].astype(jnp.bfloat16), "lat", 0).astype(jnp.float32),
    )
    d_qkv = to_half(
        jnp.concatenate(
            [
                d_queries * coarse_scale,
                d_keys[:, :half_len] + back_keys,
                d_values[:, :half_len] + back_values,
            ],
            axis=-1,
        )
    )
    grad_cqkv = jnp.dot(
        coarse_normed.reshape(-1, wide_channels).T,
        d_qkv.reshape(-1, 3 * wide_channels),
        preferred_element_type=jnp.float32,
    )
    d_coarse_normed = lax.optimization_barrier(
        to_half(jnp.dot(d_qkv, coarse_qkv.T, preferred_element_type=jnp.float32))
    )
    d_own = to_half(
        cot_windows.astype(jnp.float32)
        + norm_back(own_windows.astype(jnp.float32), d_coarse_normed.astype(jnp.float32))
    )
    d_merged = from_windows(d_own, levels, columns // 2, half_lat, WIN_LON, half_lat)
    d_fine_state, grad_merge = merge_backward(
        stacked, merge_normed, d_merged, merge_weight, channels
    )
    grad_incoming = passed_along(d_fine_state[:, :SHIFT], "lon", -1)
    d_shifted = jnp.concatenate([d_fine_state[:, SHIFT:], grad_incoming], axis=1)
    d_fine_wins, grad_fqkv, grad_fout = block_backward(
        fine_windows, fine_stash, to_windows(d_shifted, WIN_LON, WIN_LAT), fine_qkv, fine_out, HEADS
    )
    d_shift_grid = from_windows(d_fine_wins, levels, columns, latitudes, WIN_LON, WIN_LAT)
    returned = passed_along(d_shift_grid[:, columns - SHIFT :], "lon", 1)
    d_tokens = jnp.concatenate([returned, d_shift_grid[:, : columns - SHIFT]], axis=1)
    grad_factor = (
        levels * (columns // 2) * half_lat * lax.axis_size("lon") * lax.axis_size("lat")
    ) ** (-0.5)
    local_grads = (
        grad_fqkv * grad_factor,
        grad_fout * grad_factor,
        grad_merge * grad_factor,
        grad_cqkv * grad_factor,
        grad_cout * grad_factor,
    )
    shares = (
        lax.psum_scatter(local_grads[0], ("lon", "lat"), scatter_dimension=0, tiled=True),
        lax.psum_scatter(local_grads[1], ("lon", "lat"), scatter_dimension=0, tiled=True),
        lax.psum_scatter(local_grads[2], ("lon", "lat"), scatter_dimension=0, tiled=True),
        lax.psum_scatter(local_grads[3], ("lon", "lat"), scatter_dimension=0, tiled=True),
        lax.psum_scatter(local_grads[4], ("lon", "lat"), scatter_dimension=0, tiled=True),
    )
    return (coarse, d_tokens, shares[0], shares[1], shares[2], shares[3], shares[4])


def solution(mesh):
    in_specs = (P(None, "lon", "lat", None), P(None, "lon", "lat", None), P(), P(), P(), P(), P())
    out_specs = (
        P(None, "lon", "lat", None),
        P(None, "lon", "lat", None),
        P(("lon", "lat"), None),
        P(("lon", "lat"), None),
        P(("lon", "lat"), None),
        P(("lon", "lat"), None),
        P(("lon", "lat"), None),
    )
    return jax.shard_map(local, mesh=mesh, in_specs=in_specs, out_specs=out_specs, check_vma=False)
```

profile of v0, /device:TPU:0, one launch (start us, length us, event | category | flops | bytes accessed | tf_op | source)
XLA Modules:
  0.0 2362.4 jit_solution(2721301044247362514)
XLA Ops:
  8.3 3.5 collective-permute-start
  17.0 2.2 reshape.274
  26.7 4.3 fusion.76
  32.1 2.2 copy.269
  34.3 2.2 fusion.47
  36.5 2.2 copy.268
  38.7 2.2 copy.267
  40.9 5.2 fusion.77
  46.2 3.2 convolution_convert_fusion.2
  52.1 2.6 reshape.252
  54.7 2.5 copy.195
  57.2 2.8 reshape.253
  70.6 2.5 convert_bitcast_fusion
  73.8 2.9 copy.262
  76.7 3.2 reshape.283
  79.9 4.6 fusion.78
  84.7 2.5 copy.203
  87.4 2.3 reshape.271
  90.0 5.4 fusion.79
  96.3 2.7 collective-permute-start.2
  109.5 2.2 copy.271
  113.6 2.2 copy.273
  117.7 2.1 fusion.80
  120.0 8.0 fusion.56
  127.9 2.6 slice.89
  132.5 3.1 collective-permute-start.5
  135.6 3.5 multiply_reduce_fusion.1
  146.1 2.9 fusion.27
  149.0 2.3 slice.88
  152.3 2.4 copy.280
  156.6 2.4 copy.278
  161.6 5.2 fusion.43
  170.7 4.0 fusion.11
  177.0 2.9 reshape.284
  183.4 2.7 collective-permute-start.6
  187.9 3.0 convert_element_type.222
  193.3 2.6 reshape.262
  195.9 2.1 copy.275
  198.0 2.1 reshape.286
  202.1 2.5 convolution_convert_fusion.3
  204.6 2.2 copy.277
  206.9 4.7 convolution_convert_fusion
  211.6 3.4 multiply_reduce_fusion
  219.6 2.1 copy.244
  221.7 2.1 copy.242
  223.8 2.1 copy.243
  226.0 2.9 convolution_multiply_fusion.2
  228.9 3.3 fusion.10
  234.5 7.6 convolution_convert_fusion.4
  242.1 2.3 copy.251
  244.4 2.2 convert_element_type.225
  246.6 3.8 convolution_multiply_fusion.1
  253.3 2.8 convert_element_type.224
  256.2 5.7 convolution_multiply_fusion
  262.2 7.8 bitcast_multiply_fusion
  270.1 3.1 fusion.23
  276.2 2.5 copy.246
  278.7 2.1 reshape.268
  281.5 2.3 fusion.37
  286.1 2.5 collective-permute-done.7
  290.0 96.5 %all-reduce.5.cloned.1.call-done = (f32[512,1536]{1,0:T(8,128)}, f32[512,512]{1,0:T(8,128)}) async-done(((f32[512,1536]{1,0:T(8,128)}, f32[512,512]{1,0:T(8,128)}), (f32[512,1536]{1,0:T(8,128)}, f32[512,512]{1,0:T(8,128)})) %all-reduce.5.cloned.1.call-update) | async-done | bytes 4194320
  389.2 642.3 %reduce-scatter.8.cloned.1.call-done = f32[8,1024]{1,0:T(8,128)} async-done(((f32[1024,1024]{1,0:T(8,128)}), f32[8,1024]{1,0:T(8,128)}) %reduce-scatter.8.cloned.1.call-update) | async-done | bytes 32784 | tf_op jit(solution)/shard_map/reduce_scatter | solution.py:286
  1031.5 652.6 %reduce-scatter.4.cloned.1.call-done = f32[16,1024]{1,0:T(8,128)} async-done(((f32[2048,1024]{1,0:T(8,128)}), f32[16,1024]{1,0:T(8,128)}) %reduce-scatter.4.cloned.1.call-update) | async-done | bytes 65552 | tf_op jit(solution)/shard_map/reduce_scatter | solution.py:284
  1684.1 671.3 %reduce-scatter.6.cloned.1.call-done = f32[8,3072]{1,0:T(8,128)} async-done(((f32[1024,3072]{1,0:T(8,128)}), f32[8,3072]{1,0:T(8,128)}) %reduce-scatter.6.cloned.1.call-update) | async-done | bytes 98320 | tf_op jit(solution)/shard_map/reduce_scatter | solution.py:285
  (186 shorter events, 95.5 us)
Async XLA Ops:
  7.2 91.9 %copy-start = (bf16[1024,1024]{1,0:T(8,128)(2,1)S(1)}, bf16[1024,1024]{1,0:T(8,128)(2,1)}, u32[]{:S(2)}) copy-start(bf16[1024,1024]{1,0:T(8,128)(2,1)} %param.13) | copy-start | bytes 6291460
  7.2 379.2 %all-reduce.5.cloned.1.call-start = ((), (), s32[]{:S(2)}) async-start(), calls=%async_computation.6 | async-start | bytes 8388608
  8.3 6.7 collective-permute-start
  46.2 4.2 copy-start.21
  49.4 1.0 copy-start.16
  61.6 7.2 collective-permute-start.1
  69.2 0.8 copy-start.4
  70.6 2.5 copy-start.5
  84.7 2.5 copy-start.11
  90.0 9.0 copy-start.18
  96.3 11.2 collective-permute-start.2
  102.6 9.1 collective-permute-start.3
  117.7 2.2 copy-start.7
  132.5 26.5 %collective-permute-start.5 = (bf16[2,72,1024]{2,1,0:T(8,128)(2,1)}, bf16[2,72,1024]{2,1,0:T(8,128)(2,1)}, u32[]{:S(2)}, u32[]{:S(2)}) collective-permute-start(bf16[2,72,1024]{2,1,0:T(8,128)(2,1)} %copy.281), channel_id=1, source_target_pairs={{0,1},{1,0},{2,3},{3,2},{4,5},{5,4},{6,7},{7,6},{8,9},{9,8},{10,11... | collective-permute-start | bytes 884744 | tf_op jit(solution)/shard_map/ppermute | solution.py:30
  135.6 3.5 copy-start.10
  139.1 1.0 copy-start.15
  140.1 1.0 copy-start.6
  141.2 1.4 copy-start.12
  145.5 5.7 copy-start.13
  145.5 14.7 collective-permute-start.4
  159.0 2.6 copy-start.22
  160.2 6.5 copy-start.23
  161.6 5.2 copy-start.24
  161.6 5.2 copy-start.2
  166.8 1.0 copy-start.19
  170.7 4.0 copy-start.1
  179.9 6.2 copy-start.17
  181.8 0.9 copy-start.20
  183.4 8.6 collective-permute-start.6
  206.9 4.7 copy-start.25
  206.9 4.7 copy-start.26
  206.9 8.1 slice-start
  211.6 3.4 slice-start.1
  215.0 1.3 copy-start.9
  216.2 1.9 copy-start.8
  226.0 3.0 copy-start.27
  226.0 3.0 copy-start.28
  226.0 3.0 copy-start.29
  232.2 799.2 %reduce-scatter.8.cloned.1.call-start = ((), (), s32[]{:S(2)}) async-start(), calls=%async_computation.5 | async-start | bytes 4227072 | tf_op jit(solution)/shard_map/reduce_scatter | solution.py:286
  250.4 1433.6 %reduce-scatter.4.cloned.1.call-start = ((), (), s32[]{:S(2)}) async-start(), calls=%async_computation.3 | async-start | bytes 8454144 | tf_op jit(solution)/shard_map/reduce_scatter | solution.py:284
  261.9 2093.5 %reduce-scatter.6.cloned.1.call-start = ((), (), s32[]{:S(2)}) async-start(), calls=%async_computation.4 | async-start | bytes 12681216 | tf_op jit(solution)/shard_map/reduce_scatter | solution.py:285
  273.1 1.1 copy-start.14
  275.1 6.4 copy-start.3
  281.5 7.0 collective-permute-start.7
Sparse Core Ops, SparseCore 0:
  232.4 154.0 all-reduce.4
  389.3 642.0 reduce-scatter.7
  1034.5 649.4 reduce-scatter.3
  1686.9 668.4 reduce-scatter.5
where the time goes:
time: 2370 us; the launch traced here: 2360 us
  waiting for transfers between devices  2070 us (87%)
  local copies, waits for them, and re-layouts  133 us (6%)
  matrix products  101 us (4%)
  other arithmetic  29.5 us (1%)
    reduce_scatter x1, waiting for transfers between devices, local(): lax.psum_scatter(local_grads[3], ('lon', 'lat'), scatter_dimension=0, til...  671 us
    reduce_scatter x1, waiting for transfers between devices, local(): lax.psum_scatter(local_grads[2], ('lon', 'lat'), scatter_dimension=0, til...  653 us
    reduce_scatter x1, waiting for transfers between devices, local(): lax.psum_scatter(local_grads[4], ('lon', 'lat'), scatter_dimension=0, til...  642 us
    unnamed x5, waiting for transfers between devices  96.5 us
  transfers between devices with their start and end apart: 12, of which 7 were waited for; matrix products, arithmetic and copies ran while one was open for 4% of the time, Pallas kernels for 0%

commit v1 on v0

v1 whole, which is shorter than its diff:
```python
import functools

import jax
import jax.numpy as jnp
import numpy as np
from jax import lax
from jax.experimental import pallas as pl
from jax.experimental.pallas import tpu as pltpu
from jax.sharding import PartitionSpec as P

HEADS = 8
HEADS2 = 16
NORM_EPS = 1e-05
BF = jnp.bfloat16
F32 = jnp.float32
VMEM = pl.BlockSpec(memory_space=pltpu.VMEM)
MIB = 1024 * 1024


def fine_index(pair, quarter, level, lat, lon):
    return (pair * 4 + quarter) * 72 + level * 36 + lat * 6 + lon


def place_tokens():
    own = np.zeros((576, 576), np.float32)
    halo = np.zeros((576, 192), np.float32)
    for pair in range(2):
        for quarter in range(4):
            for level in range(2):
                for lat in range(6):
                    for lon in range(6):
                        row = fine_index(pair, quarter, level, lat, lon)
                        col = 6 * quarter + lon + 6
                        line = (2 * pair + level) * 6 + lat
                        if col < 24:
                            own[row, line * 24 + col] = 1
                        else:
                            halo[row, line * 8 + col - 24] = 1
    return own, halo


def place_stacked():
    body = np.zeros((576, 432), np.float32)
    tail = np.zeros((576, 144), np.float32)
    for a in range(2):
        for b in range(2):
            for pair in range(2):
                for level in range(2):
                    for i in range(12):
                        for j in range(3):
                            row = (a * 2 + b) * 144 + pair * 72 + level * 36 + i * 3 + j
                            quarter, lon, lat = i // 3, 2 * (i % 3) + a, 2 * j + b
                            inner = level * 36 + lat * 6 + lon
                            if quarter == 0:
                                tail[row, pair * 72 + inner] = 1
                            else:
                                body[row, pair * 216 + (quarter - 1) * 72 + inner] = 1
    return body, tail


def place_result():
    body = np.zeros((576, 432), np.float32)
    tail = np.zeros((576, 144), np.float32)
    for level in range(4):
        for lat in range(6):
            for lon in range(24):
                row = (level * 6 + lat) * 24 + lon
                inner = (level % 2) * 36 + lat * 6
                if lon < 6:
                    tail[row, (level // 2) * 72 + inner + lon] = 1
                else:
                    quarter = (lon - 6) // 6
                    body[row, (level // 2) * 216 + quarter * 72 + inner + lon % 6] = 1
    return body, tail


def dot(a, b):
    return lax.dot_general(a, b, (((1,), (0,)), ((), ())), preferred_element_type=F32)


def dot_nt(a, b):
    return lax.dot_general(a, b, (((1,), (1,)), ((), ())), preferred_element_type=F32)


def dot_tn(a, b):
    return lax.dot_general(a, b, (((0,), (0,)), ((), ())), preferred_element_type=F32)


def steps(count, body):
    lax.fori_loop(0, count, lambda i, carry: (body(i), carry)[1], 0)


def span(i, size):
    return pl.ds(pl.multiple_of(i * size, size), size)


def total(x):
    return jnp.sum(x, axis=-1, keepdims=True)


def norm_parts(parts):
    width = sum(p.shape[1] for p in parts)
    mean = sum(total(p) for p in parts) * (1.0 / width)
    centred = [p - mean for p in parts]
    rstd = lax.rsqrt(sum(total(c * c) for c in centred) * (1.0 / width) + NORM_EPS)
    return [c * rstd for c in centred], rstd


def norm_back(normed, rstd, upstream):
    width = sum(p.shape[1] for p in normed)
    first = sum(total(u) for u in upstream) * (1.0 / width)
    second = sum(total(u * n) for u, n in zip(upstream, normed)) * (1.0 / width)
    return [rstd * (u - first - n * second) for u, n in zip(upstream, normed)]


def half_masks(rows):
    lane = lax.broadcasted_iota(jnp.int32, (rows, 128), 1)
    low = lane < 64
    return low, jnp.where(low, 1.0, 0.0).astype(BF), jnp.where(low, 0.0, 1.0).astype(BF)


def two_heads(x, masks):
    return jnp.concatenate([x * masks[1], x * masks[2]], axis=0)


def one_row(x, masks):
    rows = x.shape[0] // 2
    return jnp.where(masks[0], x[:rows], x[rows:])


def softmax(scores):
    shifted = jnp.exp(scores - jnp.max(scores, axis=-1, keepdims=True))
    return shifted * (1.0 / total(shifted))


def attend_back(queries, keys, values, d_context, probs, weights, masks):
    d_weights = dot_nt(d_context, values)
    d_scores = (probs * (d_weights - total(d_weights * probs))).astype(BF)
    d_queries = one_row(dot(d_scores, keys), masks)
    d_keys = dot_tn(d_scores, queries)
    d_values = dot_tn(weights, d_context)
    return d_queries, d_keys, d_values


def axis_places():
    lon, lat = lax.axis_index("lon"), lax.axis_index("lat")
    return jnp.stack([lon >> 2, (lon >> 1) & 1, lon & 1, lat >> 1, lat & 1]).astype(jnp.int32)


def row_choice(place, rows, features, per_share, both_halves):
    r = lax.broadcasted_iota(jnp.int32, (rows, features), 0)
    col = lax.broadcasted_iota(jnp.int32, (rows, features), 1)
    low = r & (per_share - 1)
    r = r >> (per_share.bit_length() - 1)
    if both_halves:
        x_hi = (r & 1) ^ place[4]
        r = r >> 1
    else:
        x_hi = place[4]
    x_lo = (r & 1) ^ place[1]
    z = ((r >> 1) + place[3]) & 3
    core = ((r >> 3) & 1) ^ place[2]
    share = ((x_lo * 2 + core) * 8) + z * 2 + x_hi
    return jnp.where(share * per_share + low == col, 1.0, 0.0).astype(BF)


def fine_forward_kernel(
    tok, halo, put_own, put_halo, w_qkv, w_out, body, tail, x_out, qkv_out, ctx_out, prob_out
):
    x = dot(put_own[...], tok[...]) + dot(put_halo[...], halo[...])
    x_out[...] = x.astype(BF)
    (normed,), _ = norm_parts([x])
    normed = normed.astype(BF)
    for n in range(3):
        part = dot(normed, w_qkv[:, n * 512 : (n + 1) * 512])
        if n == 0:
            part = part * (512 // HEADS) ** (-0.5)
        qkv_out[:, n * 512 : (n + 1) * 512] = part.astype(BF)
    masks = half_masks(144)

    def window(w):
        rows = span(w, 144)
        for h in range(4):
            lanes = slice(h * 128, (h + 1) * 128)
            queries = two_heads(qkv_out[rows, lanes], masks)
            keys = qkv_out[rows, 512 + h * 128 : 512 + (h + 1) * 128]
            values = qkv_out[rows, 1024 + h * 128 : 1024 + (h + 1) * 128]
            weights = softmax(dot_nt(queries, keys)).astype(BF)
            prob_out[w * 4 + h] = weights
            ctx_out[rows, lanes] = one_row(dot(weights, values), masks).astype(BF)

    steps(4, window)
    result = x + dot(ctx_out[...], w_out[...])
    body[...] = jnp.concatenate([result[0:216], result[288:504]], axis=0).astype(BF)
    tail[...] = jnp.concatenate([result[216:288], result[504:576]], axis=0).astype(BF)


def interleave(own, far):
    return jnp.concatenate([own[:72], far[:72], own[72:], far[72:]], axis=0)


def own_rows(x):
    return jnp.concatenate([x[0:72], x[144:216]], axis=0)


def coarse_kernel(
    place_ref,
    body_own,
    tail_own,
    body_far,
    tail_far,
    put_body,
    put_tail,
    cot_own,
    cot_far,
    w_merge,
    w_qkv,
    w_out,
    coarse,
    d_merged_out,
    d_own_out,
    stacked_out,
    send,
    keep,
    merged_ref,
    normed_ref,
    qkv_ref,
    ctx_ref,
    cot_ref,
    d_ctx_ref,
    d_qkv_ref,
    left_qkv,
    left_out,
    factor,
):
    place = [place_ref[i] for i in range(5)]
    own = dot(put_body[...], body_own[...]) + dot(put_tail[...], tail_own[...])
    far = dot(put_body[...], body_far[...]) + dot(put_tail[...], tail_far[...])
    parts = [interleave(own[g * 144 : (g + 1) * 144], far[g * 144 : (g + 1) * 144]) for g in range(4)]
    for g in range(4):
        stacked_out[g] = parts[g].astype(BF)
    normed, _ = norm_parts(parts)
    merged = sum(dot(normed[g].astype(BF), w_merge[g * 512 : (g + 1) * 512, :]) for g in range(4))
    merged_ref[...] = merged.astype(BF)
    merged = merged_ref[...].astype(F32)
    (normed,), _ = norm_parts([merged])
    normed_ref[...] = normed.astype(BF)
    cot_ref[...] = interleave(cot_own[...].astype(F32), cot_far[...].astype(F32)).astype(BF)

    def project(n):
        part = dot(normed_ref[...], w_qkv[:, span(n, 512)])
        scale = jnp.where(n < 2, (1024 // HEADS2) ** (-0.5), 1.0)
        qkv_ref[:, span(n, 512)] = (part * scale).astype(BF)

    steps(6, project)

    def back_out(n):
        d_ctx_ref[:, span(n, 512)] = dot_nt(cot_ref[...], w_out[span(n, 512), :]).astype(BF)

    steps(2, back_out)
    masks = half_masks(144)

    def heads(h):
        for pair in range(2):
            rows = slice(pair * 144, (pair + 1) * 144)
            queries = two_heads(qkv_ref[rows, span(h, 128)], masks)
            keys = qkv_ref[rows, span(h + 8, 128)]
            values = qkv_ref[rows, span(h + 16, 128)]
            d_context = two_heads(d_ctx_ref[rows, span(h, 128)], masks)
            probs = softmax(dot_nt(queries, keys))
            weights = probs.astype(BF)
            ctx_ref[rows, span(h, 128)] = one_row(dot(weights, values), masks).astype(BF)
            d_queries, d_keys, d_values = attend_back(
                queries, keys, values, d_context, probs, weights, masks
            )
            d_qkv_ref[rows, span(h, 128)] = (d_queries * (1024 // HEADS2) ** (-0.5)).astype(BF)
            d_qkv_ref[rows, span(h + 8, 128)] = d_keys.astype(BF)
            d_qkv_ref[rows, span(h + 16, 128)] = d_values.astype(BF)

    steps(8, heads)

    choice = row_choice(place, 128, 256, 8, False)
    for y in range(4):
        lanes = span((place[0] + y) & 3, 256)
        block = dot_nt(choice, normed_ref[:, lanes]).astype(BF)
        other = dot_nt(choice, ctx_ref[:, lanes]).astype(BF)
        for cz in range(8):
            rows = slice((cz * 4 + y) * 16, (cz * 4 + y + 1) * 16)
            left_qkv[rows] = block[cz * 16 : (cz + 1) * 16]
            left_out[rows] = other[cz * 16 : (cz + 1) * 16]

    def grads_qkv(n):
        part = (dot(left_qkv[...], d_qkv_ref[:, span(n, 512)]) * factor).astype(BF)
        keep[:, span(n, 512)] = part[:256]
        send[:, span(n, 512)] = part[256:]

    steps(6, grads_qkv)

    def grads_out(n):
        part = (dot(left_out[...], cot_ref[:, span(n, 512)]) * factor).astype(BF)
        keep[:, span(n + 6, 512)] = part[:256]
        send[:, span(n + 6, 512)] = part[256:]

    steps(2, grads_out)

    projected = dot(ctx_ref[...], w_out[...])
    coarse[...] = own_rows(merged_ref[...].astype(F32) + projected).astype(BF)

    d_normed = jnp.zeros((288, 1024), F32)
    for n in range(3):
        d_normed = d_normed + dot_nt(
            d_qkv_ref[:, n * 1024 : (n + 1) * 1024], w_qkv[:, n * 1024 : (n + 1) * 1024]
        )
    d_normed = d_normed.astype(BF).astype(F32)
    (normed,), rstd = norm_parts([merged_ref[...].astype(F32)])
    (d_input,) = norm_back([normed], rstd, [d_normed])
    d_input = cot_ref[...].astype(F32) + d_input
    d_merged_out[...] = d_input.astype(BF)
    d_own_out[...] = own_rows(d_input).astype(BF)


def merge_back_kernel(
    place_ref,
    stacked,
    d_merged,
    d_own,
    put_body,
    put_tail,
    w_merge,
    d_body,
    d_tail,
    send,
    keep,
    normed_ref,
    d_stacked_ref,
    left,
    factor,
):
    place = [place_ref[i] for i in range(5)]
    normed, rstd = norm_parts([stacked[g].astype(F32) for g in range(4)])
    for g in range(4):
        normed_ref[g] = normed[g].astype(BF)
    upstream = []
    for g in range(4):
        part = dot_nt(d_own[...], w_merge[g * 512 : (g + 1) * 512, :])
        upstream.append(part.astype(BF).astype(F32))
    own = norm_back([own_rows(n) for n in normed], own_rows(rstd), upstream)
    for g in range(4):
        d_stacked_ref[g * 144 : (g + 1) * 144, :] = own[g].astype(BF)
    d_tail[...] = dot(put_tail[...], d_stacked_ref[...]).astype(BF)
    d_body[...] = dot(put_body[...], d_stacked_ref[...]).astype(BF)

    choice = row_choice(place, 256, 512, 16, False)
    for y in range(4):
        block = dot_nt(choice, normed_ref[(place[0] + y) & 3]).astype(BF)
        for cz in range(8):
            left[(cz * 4 + y) * 32 : (cz * 4 + y + 1) * 32] = block[cz * 32 : (cz + 1) * 32]
    for n in range(2):
        lanes = slice(n * 512, (n + 1) * 512)
        part = (dot(left[...], d_merged[:, lanes]) * factor).astype(BF)
        keep[:, lanes] = part[:512]
        send[:, lanes] = part[512:]


def fine_back_kernel(
    place_ref,
    d_body,
    d_tail,
    x_in,
    qkv,
    ctx,
    prob,
    w_qkv,
    w_out,
    body,
    tail,
    send,
    keep,
    normed_ref,
    d_res_ref,
    d_ctx_ref,
    d_qkv_ref,
    left_qkv,
    left_out,
    factor,
):
    place = [place_ref[i] for i in range(5)]
    d_own, d_far = d_body[...].astype(F32), d_tail[...].astype(F32)
    d_result = jnp.concatenate([d_own[:216], d_far[:72], d_own[216:], d_far[72:]], axis=0)
    d_res_ref[...] = d_result.astype(BF)
    d_ctx_ref[...] = dot_nt(d_res_ref[...], w_out[...]).astype(BF)
    (normed,), rstd = norm_parts([x_in[...].astype(F32)])
    normed_ref[...] = normed.astype(BF)
    masks = half_masks(144)

    def window(w):
        rows = span(w, 144)
        for h in range(4):
            lanes = slice(h * 128, (h + 1) * 128)
            queries = two_heads(qkv[rows, lanes], masks)
            keys = qkv[rows, 512 + h * 128 : 512 + (h + 1) * 128]
            values = qkv[rows, 1024 + h * 128 : 1024 + (h + 1) * 128]
            d_context = two_heads(d_ctx_ref[rows, lanes], masks)
            weights = prob[w * 4 + h]
            d_queries, d_keys, d_values = attend_back(
                queries, keys, values, d_context, weights.astype(F32), weights, masks
            )
            d_qkv_ref[rows, lanes] = (d_queries * (512 // HEADS) ** (-0.5)).astype(BF)
            d_qkv_ref[rows, 512 + h * 128 : 512 + (h + 1) * 128] = d_keys.astype(BF)
            d_qkv_ref[rows, 1024 + h * 128 : 1024 + (h + 1) * 128] = d_values.astype(BF)

    steps(4, window)

    choice = row_choice(place, 128, 128, 4, True)
    for y in range(4):
        lanes = span((place[0] + y) & 3, 128)
        block = dot_nt(choice, normed_ref[:, lanes]).astype(BF)
        other = dot_nt(choice, ctx[:, lanes]).astype(BF)
        for cz in range(8):
            rows = slice((cz * 4 + y) * 16, (cz * 4 + y + 1) * 16)
            left_qkv[rows] = block[cz * 16 : (cz + 1) * 16]
            left_out[rows] = other[cz * 16 : (cz + 1) * 16]

    def grads_qkv(n):
        part = (dot(left_qkv[...], d_qkv_ref[:, span(n, 512)]) * factor).astype(BF)
        keep[:, span(n, 512)] = part[:256]
        send[:, span(n, 512)] = part[256:]

    steps(3, grads_qkv)
    part = (dot(left_out[...], d_res_ref[...]) * factor).astype(BF)
    keep[:, 1536:] = part[:256]
    send[:, 1536:] = part[256:]

    d_normed = dot_nt(d_qkv_ref[...], w_qkv[...]).astype(BF).astype(F32)
    (d_input,) = norm_back([normed], rstd, [d_normed])
    d_input = d_res_ref[...].astype(F32) + d_input
    body[...] = jnp.concatenate([d_input[0:216], d_input[288:504]], axis=0).astype(BF)
    tail[...] = jnp.concatenate([d_input[216:288], d_input[504:576]], axis=0).astype(BF)


def place_result_kernel(body, tail, put_body, put_tail, out):
    out[...] = (dot(put_body[...], body[...]) + dot(put_tail[...], tail[...])).astype(BF)


def call(kernel, outs, scratch=(), scalars=0, limit=56):
    def run(*args):
        in_specs = [pl.BlockSpec(memory_space=pltpu.SMEM)] * scalars + [VMEM] * (len(args) - scalars)
        return pl.pallas_call(
            kernel,
            out_shape=[jax.ShapeDtypeStruct(shape, dtype) for shape, dtype in outs],
            in_specs=in_specs,
            out_specs=[VMEM] * len(outs),
            scratch_shapes=[pltpu.VMEM(shape, dtype) for shape, dtype in scratch],
            compiler_params=pltpu.CompilerParams(vmem_limit_bytes=limit * MIB),
        )(*args)

    return run


def route(move):
    pairs = []
    for source in range(128):
        lon, lat = divmod(source, 8)
        y, x_lo, core, z, x_hi = move(lon >> 2, (lon >> 1) & 1, lon & 1, lat >> 1, lat & 1)
        pairs.append((source, (((y & 3) * 2 + x_lo) * 2 + core) * 8 + (z & 3) * 2 + x_hi))
    return pairs


def send_core(x):
    return lax.ppermute(x, ("lon", "lat"), route(lambda y, xl, c, z, xh: (y, xl, 1 - c, z, xh)))


def send_z(x, d):
    return lax.ppermute(x, ("lon", "lat"), route(lambda y, xl, c, z, xh: (y, xl, c, z + d, xh)))


def send_y(x, d):
    return lax.ppermute(x, ("lon", "lat"), route(lambda y, xl, c, z, xh: (y + d, xl, c, z, xh)))


def send_x_lo(x):
    return lax.ppermute(x, ("lon", "lat"), route(lambda y, xl, c, z, xh: (y, 1 - xl, c, z, xh)))


def send_x_hi(x):
    return lax.ppermute(x, ("lon", "lat"), route(lambda y, xl, c, z, xh: (y, xl, c, z, 1 - xh)))


def send_lon(x, step, partner):
    pairs = []
    for lon in range(16):
        for lat in range(8):
            pairs.append((lon * 8 + lat, (lon + step) % 16 * 8 + (lat ^ partner)))
    return lax.ppermute(x, ("lon", "lat"), pairs)


def add_split_kernel(keep, got, *pieces):
    half = keep.shape[3] // 2
    for d in range(4):
        first = keep[d, :, :, :half].astype(F32) + got[d, :, :, :half].astype(F32)
        pieces[d][...] = first.astype(BF)
        last = keep[:, d, :, half:].astype(F32) + got[:, d, :, half:].astype(F32)
        pieces[4 + d][...] = last.astype(BF)


def add_four_kernel(*refs):
    sums = [sum(r[...].astype(F32) for r in refs[s * 4 : s * 4 + 4]).astype(BF) for s in range(2)]
    for s in range(2):
        for d in range(4):
            refs[8 + s * 4 + d][...] = sums[s][d]


def add_last_kernel(*refs):
    sums = [sum(r[...].astype(F32) for r in refs[s * 4 : s * 4 + 4]).astype(BF) for s in range(2)]
    both = jnp.concatenate(sums, axis=1)
    rows = both.shape[0] // 2
    refs[8][...] = both[:rows]
    refs[9][...] = both[rows:]


def spread_core(send, keep, rows, columns):
    return keep.reshape(4, 4, rows, columns), send_core(send).reshape(4, 4, rows, columns)


def reduce_first(keep, got):
    rows, columns = keep.shape[2:]
    pieces = call(add_split_kernel, [((4, rows, columns // 2), BF)] * 8)(keep, got)
    return (
        [pieces[0]] + [send_z(pieces[d], d) for d in (1, 2, 3)],
        [pieces[4]] + [send_y(pieces[4 + d], d) for d in (1, 2, 3)],
    )


def reduce_second(first, last):
    shape = first[0].shape[1:]
    pieces = call(add_four_kernel, [(shape, BF)] * 8)(*first, *last)
    return (
        [pieces[0]] + [send_y(pieces[d], d) for d in (1, 2, 3)],
        [pieces[4]] + [send_z(pieces[4 + d], d) for d in (1, 2, 3)],
    )


def reduce_third(first, last):
    rows, columns = first[0].shape
    keep, send = call(add_last_kernel, [((rows // 2, columns * 2), BF)] * 2)(*first, *last)
    return keep, send_x_lo(send)


def local(tokens, cotangent, fine_qkv, fine_out, merge_weight, coarse_qkv, coarse_out):
    factor = (144 * lax.axis_size("lon") * lax.axis_size("lat")) ** (-0.5)
    place = axis_places()
    put_own, put_halo = (jnp.asarray(a, BF) for a in place_tokens())
    stack_body, stack_tail = place_stacked()
    back_body, back_tail = (jnp.asarray(a, BF) for a in place_result())

    tok = tokens.transpose(0, 2, 1, 3)
    halo = send_lon(tok[:, :, :8], -1, 0).reshape(192, 512)
    cot_own = cotangent.reshape(144, 1024)
    cot_far = send_lon(cot_own, 0, 1)

    body, tail, x_fine, qkv_fine, ctx_fine, prob_fine = call(
        fine_forward_kernel,
        [
            ((432, 512), BF),
            ((144, 512), BF),
            ((576, 512), BF),
            ((576, 1536), BF),
            ((576, 512), BF),
            ((16, 288, 144), BF),
        ],
    )(tok.reshape(576, 512), halo, put_own, put_halo, fine_qkv, fine_out)
    tail_own = send_lon(tail, 1, 0)
    tail_far = send_lon(tail, 1, 1)
    body_far = send_lon(body, 0, 1)

    coarse, d_merged, d_merged_own, stacked, send_a, keep_a = call(
        functools.partial(coarse_kernel, factor=factor),
        [
            ((144, 1024), BF),
            ((288, 1024), BF),
            ((144, 1024), BF),
            ((4, 288, 512), BF),
            ((256, 4096), BF),
            ((256, 4096), BF),
        ],
        [
            ((288, 1024), BF),
            ((288, 1024), BF),
            ((288, 3072), BF),
            ((288, 1024), BF),
            ((288, 1024), BF),
            ((288, 1024), BF),
            ((288, 3072), BF),
            ((512, 288), BF),
            ((512, 288), BF),
        ],
        scalars=1,
    )(
        place,
        body,
        tail_own,
        body_far,
        tail_far,
        jnp.asarray(stack_body, BF),
        jnp.asarray(stack_tail, BF),
        cot_own,
        cot_far,
        merge_weight,
        coarse_qkv,
        coarse_out,
    )
    core_a = spread_core(send_a, keep_a, 16, 4096)

    d_body, d_tail, send_m, keep_m = call(
        functools.partial(merge_back_kernel, factor=factor),
        [((432, 512), BF), ((144, 512), BF), ((512, 1024), BF), ((512, 1024), BF)],
        [((4, 288, 512), BF), ((576, 512), BF), ((1024, 288), BF)],
        scalars=1,
    )(
        place,
        stacked,
        d_merged,
        d_merged_own,
        jnp.asarray(stack_body.T, BF),
        jnp.asarray(stack_tail.T, BF),
        merge_weight,
    )
    d_tail_east = send_lon(d_tail, -1, 0)
    core_m = spread_core(send_m, keep_m, 32, 1024)
    first_a = reduce_first(*core_a)
    first_m = reduce_first(*core_m)

    d_in_body, d_in_tail, send_f, keep_f = call(
        functools.partial(fine_back_kernel, factor=factor),
        [((432, 512), BF), ((144, 512), BF), ((256, 2048), BF), ((256, 2048), BF)],
        [
            ((576, 512), BF),
            ((576, 512), BF),
            ((576, 512), BF),
            ((576, 1536), BF),
            ((512, 576), BF),
            ((512, 576), BF),
        ],
        scalars=1,
    )(place, d_body, d_tail_east, x_fine, qkv_fine, ctx_fine, prob_fine, fine_qkv, fine_out)
    core_f = spread_core(send_f, keep_f, 16, 2048)
    d_in_west = send_lon(d_in_tail, 1, 0)
    second_a = reduce_second(*first_a)
    second_m = reduce_second(*first_m)
    first_f = reduce_first(*core_f)
    (d_tokens,) = call(place_result_kernel, [((576, 512), BF)])(
        d_in_body, d_in_west, back_body, back_tail
    )
    keep_a, got_a = reduce_third(*second_a)
    keep_m, got_m = reduce_third(*second_m)
    keep_f, got_f = reduce_third(*reduce_second(*first_f))
    share_a = keep_a.astype(F32) + got_a.astype(F32)
    share_m = keep_m.astype(F32) + got_m.astype(F32)
    share_f = (keep_f.astype(F32) + got_f.astype(F32)).reshape(2, 4, 2048)
    share_f = share_f[0] + send_x_hi(share_f[1].astype(BF)).astype(F32)
    return (
        coarse.reshape(4, 12, 3, 1024),
        d_tokens.reshape(4, 6, 24, 512).transpose(0, 2, 1, 3),
        share_f[:, :1536],
        share_f[:, 1536:],
        share_m,
        share_a[:, :3072],
        share_a[:, 3072:],
    )


def solution(mesh):
    grid_spec = P(None, "lon", "lat", None)
    rows_spec = P(("lon", "lat"), None)
    return jax.shard_map(
        local,
        mesh=mesh,
        in_specs=(grid_spec, grid_spec, P(), P(), P(), P(), P()),
        out_specs=(grid_spec, grid_spec) + (rows_spec,) * 5,
        check_vma=False,
    )
```

time: 2370 us -> 219 us (0.09)
  waiting for transfers between devices: 2070 us -> 39.8 us
  local copies, waits for them, and re-layouts: 133 us -> 14 us
  matrix products: 101 us -> 0 us
  Pallas kernels: 0 us -> 90.9 us
  starting transfers between devices: 14.7 us -> 67.5 us
  other arithmetic: 29.5 us -> 1.52 us
    reduce_scatter x3 -> x0, waiting for transfers between devices: 1970 us -> none  [the longest x1 671 us: local(): lax.psum_scatter(local_grads[3], ('lon', 'lat'), scatter_dimension=0, til...]
    unnamed x5 -> x0, waiting for transfers between devices: 96.5 us -> none
    dot_general x26 -> x0, matrix products: 95.8 us -> none  [the longest x2 12.7 us: attend_back(): jnp.einsum('bhqk,bqhd->bkhd', attn_weights, d_ctx_heads, preferred_elemen...]
    pallas_call x0 -> x14, Pallas kernels: none -> 90.9 us  [run(): pl.pallas_call(kernel, out_shape=[jax.ShapeDtypeStruct(shape, dtype) for...]
    ppermute x8 -> x50, starting transfers between devices: 14 us -> 67.5 us  [the longest x18 28.6 us: send_z(): lax.ppermute(x, ('lon', 'lat'), route(lambda y, xl, c, z, xh: (y, xl, c,...]
    reshape x18 -> x2, local copies, waits for them, and re-layouts: 39.5 us -> 0.43 us  [the longest x1 0.25 us: local(): cot_own = cotangent.reshape(144, 1024)]
    ppermute x8 -> x50, waiting for transfers between devices: 6.47 us -> 39.8 us  [the longest x7 25.4 us: send_lon(): return lax.ppermute(x, ('lon', 'lat'), pairs)]
    convert_element_type x16 -> x0, local copies, waits for them, and re-layouts: 33 us -> none  [the longest x8 15.1 us: to_half(): return tensor.astype(jnp.bfloat16)]
  transfers between devices with their start and end apart: 12 -> 50, of which waited for: 7 -> 14; matrix products, arithmetic and copies ran while one was open for 4% -> 2% of each run, Pallas kernels for 0% -> 22%
where the time goes in v1:
time: 219 us; the launch traced here: 215 us
  Pallas kernels  90.9 us (42%)
  starting transfers between devices  67.5 us (31%)
  waiting for transfers between devices  39.8 us (18%)
  local copies, waits for them, and re-layouts  14 us (6%)
    pallas_call x14, Pallas kernels, run(): pl.pallas_call(kernel, out_shape=[jax.ShapeDtypeStruct(shape, dtype) for...  90.9 us
    ppermute x18, starting transfers between devices, send_z(): lax.ppermute(x, ('lon', 'lat'), route(lambda y, xl, c, z, xh: (y, xl, c,...  28.6 us
    ppermute x7, waiting for transfers between devices, send_lon(): return lax.ppermute(x, ('lon', 'lat'), pairs)  25.4 us
    ppermute x18, starting transfers between devices, send_y(): lax.ppermute(x, ('lon', 'lat'), route(lambda y, xl, c, z, xh: (y + d, xl,...  23.1 us
    unnamed x124, local copies, waits for them, and re-layouts  9.56 us
    ppermute x7, starting transfers between devices, send_lon(): return lax.ppermute(x, ('lon', 'lat'), pairs)  8.76 us
    ppermute x18, waiting for transfers between devices, send_z(): lax.ppermute(x, ('lon', 'lat'), route(lambda y, xl, c, z, xh: (y, xl, c,...  8.11 us
  transfers between devices with their start and end apart: 50, of which 14 were waited for; matrix products, arithmetic and copies ran while one was open for 2% of the time, Pallas kernels for 22%

profile of v1, /device:TPU:0, one launch (start us, length us, event | category | flops | bytes accessed | tf_op | source)
XLA Modules:
  0.0 215.3 jit_solution(11683290854441601586)
XLA Ops:
  0.6 1.0 slice.31
  1.6 3.5 %collective-permute-start = (bf16[4,6,8,512]{3,2,1,0:T(8,128)(2,1)S(1)}, bf16[4,6,8,512]{3,2,1,0:T(8,128)(2,1)S(1)}, u32[]{:S(2)}, u32[]{:S(2)}) collective-permute-start(bf16[4,6,8,512]{3,2,1,0:T(8,128)(2,1)S(1)} %slice.31), channel_id=1, source_target_pairs={{0,120},{1,121},{2,122},{3,123},{4,124},{5,125},{6,126},{7,127},{8... | collective-permute-start | bytes 589832 | tf_op jit(solution)/shard_map/ppermute | solution.py:494
  5.2 3.2 %collective-permute-done = bf16[4,6,8,512]{3,2,1,0:T(8,128)(2,1)S(1)} collective-permute-done((bf16[4,6,8,512]{3,2,1,0:T(8,128)(2,1)S(1)}, bf16[4,6,8,512]{3,2,1,0:T(8,128)(2,1)S(1)}, u32[]{:S(2)}, u32[]{:S(2)}) %collective-permute-start) | collective-permute-done | bytes 196640 | tf_op jit(solution)/shard_map/ppermute | solution.py:494
  9.0 10.6 %shard_map.198 = (bf16[432,512]{1,0:T(8,128)(2,1)}, bf16[144,512]{1,0:T(8,128)(2,1)}, bf16[576,512]{1,0:T(8,128)(2,1)}, bf16[576,1536]{1,0:T(8,128)(2,1)}, bf16[...) custom-call(bf16[576,512]{1,0:T(8,128)(2,1)} %bitcast.25, bf16[192,512]{1,0:T(8,128)(2,1)} %bitcast.27, ...), custom_call_target="tpu_custom_call" | custom-call | tf_op jit(solution)/shard_map/pallas_call | solution.py:448
  19.7 2.7 %collective-permute-start.2 = (bf16[432,512]{1,0:T(8,128)(2,1)}, bf16[432,512]{1,0:T(8,128)(2,1)S(1)}, u32[]{:S(2)}, u32[]{:S(2)}) collective-permute-start(bf16[432,512]{1,0:T(8,128)(2,1)} %get-tuple-element.81.body_own), channel_id=1, source_target_pairs={{0,1},{1,0},{2,3},{3,2},{4,5},{5,4},{6,7},{7,6},{8,9},{9,8},{10,11... | collective-permute-start | bytes 1327112 | tf_op jit(solution)/shard_map/ppermute | solution.py:494
  22.9 0.9 collective-permute-start.4
  24.9 14.9 %collective-permute-done.4.cot_far = bf16[144,1024]{1,0:T(8,128)(2,1)S(1)} collective-permute-done((bf16[144,1024]{1,0:T(8,128)(2,1)S(1)}, bf16[144,1024]{1,0:T(8,128)(2,1)S(1)}, u32[]{:S(2)}, u32[]{:S(2)}) %collective-permute-start.4) | collective-permute-done | bytes 294944 | tf_op jit(solution)/shard_map/ppermute | solution.py:494
  39.8 4.2 %collective-permute-done.3.tail_far = bf16[144,512]{1,0:T(8,128)(2,1)S(1)} collective-permute-done((bf16[144,512]{1,0:T(8,128)(2,1)}, bf16[144,512]{1,0:T(8,128)(2,1)S(1)}, u32[]{:S(2)}, u32[]{:S(2)}) %collective-permute-start.3) | collective-permute-done | bytes 147488 | tf_op jit(solution)/shard_map/ppermute | solution.py:494
  45.6 32.8 %shard_map.199 = (bf16[144,1024]{1,0:T(8,128)(2,1)}, bf16[288,1024]{1,0:T(8,128)(2,1)}, bf16[144,1024]{1,0:T(8,128)(2,1)}, bf16[4,288,512]{2,1,0:T(8,128)(2,1)},...) custom-call(s32[5]{0:T(128)} %stack.23.place_ref, bf16[432,512]{1,0:T(8,128)(2,1)} %get-tuple-element.81.body_own, ...), custom_call_target="tpu_custom_call" | custom-call | tf_op jit(solution)/shard_map/pallas_call | solution.py:448
  78.4 8.7 %shard_map.200 = (bf16[432,512]{1,0:T(8,128)(2,1)}, bf16[144,512]{1,0:T(8,128)(2,1)}, bf16[512,1024]{1,0:T(8,128)(2,1)}, bf16[512,1024]{1,0:T(8,128)(2,1)}) custom-call(s32[5]{0:T(128)} %stack.23.place_ref, bf16[4,288,512]{2,1,0:T(8,128)(2,1)} %get-tuple-element.84.stacked, bf16[288,1024]{1,0:T(8,128)(2,1)} %get-tuple-element.85.d_merged, ...), custom_call_target="tpu_custom_call" | custom-call | tf_op jit(solution)/shard_map/pallas_call | solution.py:448
  87.6 1.0 collective-permute-start.5
  88.5 3.0 %collective-permute-done.5.d_tail = bf16[144,512]{1,0:T(8,128)(2,1)S(1)} collective-permute-done((bf16[144,512]{1,0:T(8,128)(2,1)}, bf16[144,512]{1,0:T(8,128)(2,1)S(1)}, u32[]{:S(2)}, u32[]{:S(2)}) %collective-permute-start.5) | collective-permute-done | bytes 147488 | tf_op jit(solution)/shard_map/ppermute | solution.py:494
  92.2 16.1 %shard_map.201 = (bf16[432,512]{1,0:T(8,128)(2,1)}, bf16[144,512]{1,0:T(8,128)(2,1)}, bf16[256,2048]{1,0:T(8,128)(2,1)}, bf16[256,2048]{1,0:T(8,128)(2,1)}) custom-call(s32[5]{0:T(128)} %stack.23.place_ref, bf16[432,512]{1,0:T(8,128)(2,1)} %get-tuple-element.87.d_body, bf16[144,512]{1,0:T(8,128)(2,1)} %copy-done.18, ...), custom_call_target="tpu_custom_call" | custom-call | tf_op jit(solution)/shard_map/pallas_call | solution.py:448
  108.3 1.2 collective-permute-start.7
  109.5 1.1 copy-done.3
  110.5 2.5 %shard_map.206 = (bf16[4,32,512]{2,1,0:T(8,128)(2,1)}, bf16[4,32,512]{2,1,0:T(8,128)(2,1)}, bf16[4,32,512]{2,1,0:T(8,128)(2,1)}, bf16[4,32,512]{2,1,0:T(8,128)(2...) custom-call(bf16[4,4,32,1024]{3,2,1,0:T(8,128)(2,1)} %bitcast.22, ...), custom_call_target="tpu_custom_call" | custom-call | tf_op jit(solution)/shard_map/pallas_call | solution.py:448
  113.1 1.9 collective-permute-start.23
  115.0 3.6 %collective-permute-start.24 = (bf16[4,32,512]{2,1,0:T(8,128)(2,1)}, bf16[4,32,512]{2,1,0:T(8,128)(2,1)S(1)}, u32[]{:S(2)}, u32[]{:S(2)}) collective-permute-start(bf16[4,32,512]{2,1,0:T(8,128)(2,1)} %get-tuple-element.119), channel_id=1, source_target_pairs={{0,4},{1,5},{2,6},{3,7},{4,0},{5,1},{6,2},{7,3},{8,12},{9,13},{10,... | collective-permute-start | bytes 393224 | tf_op jit(solution)/shard_map/ppermute | solution.py:474
  118.6 1.0 collective-permute-start.25
  119.6 1.4 collective-permute-done.23.refs_1_
  121.0 4.0 %collective-permute-done.24.refs_2_ = bf16[4,32,512]{2,1,0:T(8,128)(2,1)S(1)} collective-permute-done((bf16[4,32,512]{2,1,0:T(8,128)(2,1)}, bf16[4,32,512]{2,1,0:T(8,128)(2,1)S(1)}, u32[]{:S(2)}, u32[]{:S(2)}) %collective-permute-start.24) | collective-permute-done | bytes 131104 | tf_op jit(solution)/shard_map/ppermute | solution.py:474
  126.3 1.0 copy-done.2
  127.2 2.5 %shard_map.203 = (bf16[4,16,1024]{2,1,0:T(8,128)(2,1)}, bf16[4,16,1024]{2,1,0:T(8,128)(2,1)}, bf16[4,16,1024]{2,1,0:T(8,128)(2,1)}, bf16[4,16,1024]{2,1,0:T(8,12...) custom-call(bf16[4,4,16,2048]{3,2,1,0:T(8,128)(2,1)} %bitcast.20, ...), custom_call_target="tpu_custom_call" | custom-call | tf_op jit(solution)/shard_map/pallas_call | solution.py:448
  129.8 0.9 collective-permute-start.8
  130.7 1.3 collective-permute-done.27.refs_6_
  132.0 1.9 collective-permute-start.9
  134.6 2.0 shard_map.207
  137.0 1.3 copy-done
  138.4 3.7 %shard_map.209 = (bf16[4,16,2048]{2,1,0:T(8,128)(2,1)}, bf16[4,16,2048]{2,1,0:T(8,128)(2,1)}, bf16[4,16,2048]{2,1,0:T(8,128)(2,1)}, bf16[4,16,2048]{2,1,0:T(8,12...) custom-call(bf16[4,4,16,4096]{3,2,1,0:T(8,128)(2,1)} %bitcast.18, ...), custom_call_target="tpu_custom_call" | custom-call | tf_op jit(solution)/shard_map/pallas_call | solution.py:448
  142.1 1.2 collective-permute-start.37
  143.3 2.1 collective-permute-start.10
  146.1 3.7 %collective-permute-start.12 = (bf16[4,16,1024]{2,1,0:T(8,128)(2,1)S(1)}, bf16[4,16,1024]{2,1,0:T(8,128)(2,1)S(1)}, u32[]{:S(2)}, u32[]{:S(2)}) collective-permute-start(bf16[4,16,1024]{2,1,0:T(8,128)(2,1)S(1)} %copy-done.53), channel_id=1, source_target_pairs={{0,64},{1,65},{2,66},{3,67},{4,68},{5,69},{6,70},{7,71},{8,72},{9,... | collective-permute-start | bytes 393224 | tf_op jit(solution)/shard_map/ppermute | solution.py:478
  150.2 1.7 collective-permute-start.30
  151.9 2.9 %collective-permute-start.31 = (bf16[32,512]{1,0:T(8,128)(2,1)S(1)}, bf16[32,512]{1,0:T(8,128)(2,1)S(1)}, u32[]{:S(2)}, u32[]{:S(2)}) collective-permute-start(bf16[32,512]{1,0:T(8,128)(2,1)S(1)} %copy-done.59), channel_id=1, source_target_pairs={{0,96},{1,97},{2,98},{3,99},{4,100},{5,101},{6,102},{7,103},{8,104... | collective-permute-start | bytes 98312 | tf_op jit(solution)/shard_map/ppermute | solution.py:478
  154.8 1.3 collective-permute-done.12.refs_6_
  156.4 1.8 collective-permute-start.33
  158.3 2.0 shard_map.204
  160.3 2.0 collective-permute-start.34
  162.5 2.4 %collective-permute-start.15 = (bf16[16,1024]{1,0:T(8,128)(2,1)}, bf16[16,1024]{1,0:T(8,128)(2,1)S(1)}, u32[]{:S(2)}, u32[]{:S(2)}) collective-permute-start(bf16[16,1024]{1,0:T(8,128)(2,1)} %get-tuple-element.107), channel_id=1, source_target_pairs={{0,64},{1,65},{2,66},{3,67},{4,68},{5,69},{6,70},{7,71},{8,72},{9,... | collective-permute-start | bytes 98312 | tf_op jit(solution)/shard_map/ppermute | solution.py:478
  164.9 0.9 collective-permute-start.16
  165.8 0.9 collective-permute-start.17
  166.6 1.0 collective-permute-done.14.refs_1_
  167.7 2.4 %collective-permute-start.18 = (bf16[16,1024]{1,0:T(8,128)(2,1)}, bf16[16,1024]{1,0:T(8,128)(2,1)S(1)}, u32[]{:S(2)}, u32[]{:S(2)}) collective-permute-start(bf16[16,1024]{1,0:T(8,128)(2,1)} %get-tuple-element.111), channel_id=1, source_target_pairs={{0,4},{1,5},{2,6},{3,7},{4,0},{5,1},{6,2},{7,3},{8,12},{9,13},{10,... | collective-permute-start | bytes 98312 | tf_op jit(solution)/shard_map/ppermute | solution.py:474
  170.8 1.1 collective-permute-start.38
  171.9 2.9 %collective-permute-start.39 = (bf16[4,16,2048]{2,1,0:T(8,128)(2,1)}, bf16[4,16,2048]{2,1,0:T(8,128)(2,1)S(1)}, u32[]{:S(2)}, u32[]{:S(2)}) collective-permute-start(bf16[4,16,2048]{2,1,0:T(8,128)(2,1)} %get-tuple-element.140), channel_id=1, source_target_pairs={{0,6},{1,7},{2,0},{3,1},{4,2},{5,3},{6,4},{7,5},{8,14},{9,15},{10,... | collective-permute-start | bytes 786440 | tf_op jit(solution)/shard_map/ppermute | solution.py:474
  174.8 2.7 %collective-permute-start.41 = (bf16[4,16,2048]{2,1,0:T(8,128)(2,1)}, bf16[4,16,2048]{2,1,0:T(8,128)(2,1)S(1)}, u32[]{:S(2)}, u32[]{:S(2)}) collective-permute-start(bf16[4,16,2048]{2,1,0:T(8,128)(2,1)} %get-tuple-element.143), channel_id=1, source_target_pairs={{0,64},{1,65},{2,66},{3,67},{4,68},{5,69},{6,70},{7,71},{8,72},{9,... | collective-permute-start | bytes 786440 | tf_op jit(solution)/shard_map/ppermute | solution.py:478
  177.5 0.9 collective-permute-start.42
  178.4 1.5 shard_map.205
  180.0 1.8 collective-permute-start.20
  182.0 1.0 copy.25
  183.0 2.8 %shard_map.202 = bf16[576,512]{1,0:T(8,128)(2,1)} custom-call(bf16[432,512]{1,0:T(8,128)(2,1)} %get-tuple-element.93.body, bf16[144,512]{1,0:T(8,128)(2,1)} %copy-done.17, bf16[576,432]{1,0:T(8,128)(2,1)} %constant.31.clone.put_body, bf16[576,144]{1,0:T(8,128)(2,1)} %constant.32.clone.put_tail), custom_call_target="tpu_custom_call" | custom-call | tf_op jit(solution)/shard_map/pallas_call | solution.py:448
  185.8 1.5 shard_map.208
  188.6 2.4 %shard_map.210 = (bf16[16,2048]{1,0:T(8,128)(2,1)}, bf16[16,2048]{1,0:T(8,128)(2,1)}, bf16[16,2048]{1,0:T(8,128)(2,1)}, bf16[16,2048]{1,0:T(8,128)(2,1)}, bf16[1...) custom-call(bf16[4,16,2048]{2,1,0:T(8,128)(2,1)} %get-tuple-element.137.refs, ...), custom_call_target="tpu_custom_call" | custom-call | tf_op jit(solution)/shard_map/pallas_call | solution.py:448
  191.0 1.1 collective-permute-start.43
  192.1 1.5 collective-permute-start.44
  193.7 2.4 %collective-permute-start.21 = (bf16[4,2048]{1,0:T(4,128)(2,1)S(1)}, bf16[4,2048]{1,0:T(4,128)(2,1)S(1)}, u32[]{:S(2)}, u32[]{:S(2)}) collective-permute-start(bf16[4,2048]{1,0:T(4,128)(2,1)S(1)} %slice.40), channel_id=1, source_target_pairs={{0,1},{1,0},{2,3},{3,2},{4,5},{5,4},{6,7},{7,6},{8,9},{9,8},{10,11... | collective-permute-start | bytes 49160 | tf_op jit(solution)/shard_map/ppermute | solution.py:486
  196.1 2.5 %collective-permute-start.45 = (bf16[16,2048]{1,0:T(8,128)(2,1)}, bf16[16,2048]{1,0:T(8,128)(2,1)S(1)}, u32[]{:S(2)}, u32[]{:S(2)}) collective-permute-start(bf16[16,2048]{1,0:T(8,128)(2,1)} %get-tuple-element.148), channel_id=1, source_target_pairs={{0,96},{1,97},{2,98},{3,99},{4,100},{5,101},{6,102},{7,103},{8,104... | collective-permute-start | bytes 196616 | tf_op jit(solution)/shard_map/ppermute | solution.py:478
  198.6 1.1 collective-permute-start.46
  199.7 1.4 collective-permute-start.47
  201.1 1.4 collective-permute-start.48
  203.2 1.1 collective-permute-done.46.refs_5_
  204.3 1.4 collective-permute-done.47.refs_6_
  206.5 1.7 shard_map.211
  210.2 2.5 %collective-permute-done.49 = bf16[8,4096]{1,0:T(8,128)(2,1)S(1)} collective-permute-done((bf16[8,4096]{1,0:T(8,128)(2,1)}, bf16[8,4096]{1,0:T(8,128)(2,1)S(1)}, u32[]{:S(2)}, u32[]{:S(2)}) %collective-permute-start.49) | collective-permute-done | bytes 65568 | tf_op jit(solution)/shard_map/ppermute | solution.py:482
  (187 shorter events, 16.5 us)
Async XLA Ops:
  0.6 21.8 %copy-start.5 = (bf16[4,12,3,1024]{3,0,2,1:T(4,128)(2,1)S(1)}, bf16[4,12,3,1024]{3,0,2,1:T(4,128)(2,1)}, u32[]{:S(2)}) copy-start(bf16[4,12,3,1024]{3,0,2,1:T(4,128)(2,1)} %param.16) | copy-start | bytes 884740
  1.6 6.7 %collective-permute-start = (bf16[4,6,8,512]{3,2,1,0:T(8,128)(2,1)S(1)}, bf16[4,6,8,512]{3,2,1,0:T(8,128)(2,1)S(1)}, u32[]{:S(2)}, u32[]{:S(2)}) collective-permute-start(bf16[4,6,8,512]{3,2,1,0:T(8,128)(2,1)S(1)} %slice.31), channel_id=1, source_target_pairs={{0,120},{1,121},{2,122},{3,123},{4,124},{5,125},{6,126},{7,127},{8... | collective-permute-start | bytes 589832 | tf_op jit(solution)/shard_map/ppermute | solution.py:494
  19.7 24.5 %collective-permute-start.2 = (bf16[432,512]{1,0:T(8,128)(2,1)}, bf16[432,512]{1,0:T(8,128)(2,1)S(1)}, u32[]{:S(2)}, u32[]{:S(2)}) collective-permute-start(bf16[432,512]{1,0:T(8,128)(2,1)} %get-tuple-element.81.body_own), channel_id=1, source_target_pairs={{0,1},{1,0},{2,3},{3,2},{4,5},{5,4},{6,7},{7,6},{8,9},{9,8},{10,11... | collective-permute-start | bytes 1327112 | tf_op jit(solution)/shard_map/ppermute | solution.py:494
  22.8 21.3 %copy-start.1 = (bf16[144,1024]{1,0:T(8,128)(2,1)}, bf16[144,1024]{1,0:T(8,128)(2,1)S(1)}, u32[]{:S(2)}) copy-start(bf16[144,1024]{1,0:T(8,128)(2,1)S(1)} %reshape.54.cot_own) | copy-start | bytes 884740
  22.9 16.9 %collective-permute-start.4 = (bf16[144,1024]{1,0:T(8,128)(2,1)S(1)}, bf16[144,1024]{1,0:T(8,128)(2,1)S(1)}, u32[]{:S(2)}, u32[]{:S(2)}) collective-permute-start(bf16[144,1024]{1,0:T(8,128)(2,1)S(1)} %reshape.54.cot_own), channel_id=1, source_target_pairs={{0,1},{1,0},{2,3},{3,2},{4,5},{5,4},{6,7},{7,6},{8,9},{9,8},{10,11... | collective-permute-start | bytes 884744 | tf_op jit(solution)/shard_map/ppermute | solution.py:494
  23.7 20.3 %collective-permute-start.3 = (bf16[144,512]{1,0:T(8,128)(2,1)}, bf16[144,512]{1,0:T(8,128)(2,1)S(1)}, u32[]{:S(2)}, u32[]{:S(2)}) collective-permute-start(bf16[144,512]{1,0:T(8,128)(2,1)} %get-tuple-element.82), channel_id=1, source_target_pairs={{0,9},{1,8},{2,11},{3,10},{4,13},{5,12},{6,15},{7,14},{8,17},{9,16... | collective-permute-start | bytes 442376 | tf_op jit(solution)/shard_map/ppermute | solution.py:494
  24.2 20.0 %collective-permute-start.1 = (bf16[144,512]{1,0:T(8,128)(2,1)}, bf16[144,512]{1,0:T(8,128)(2,1)S(1)}, u32[]{:S(2)}, u32[]{:S(2)}) collective-permute-start(bf16[144,512]{1,0:T(8,128)(2,1)} %get-tuple-element.82), channel_id=1, source_target_pairs={{0,8},{1,9},{2,10},{3,11},{4,12},{5,13},{6,14},{7,15},{8,16},{9,17... | collective-permute-start | bytes 442376 | tf_op jit(solution)/shard_map/ppermute | solution.py:494
  78.4 58.6 %collective-permute-start.36 = (bf16[256,4096]{1,0:T(8,128)(2,1)}, bf16[256,4096]{1,0:T(8,128)(2,1)S(1)}, u32[]{:S(2)}, u32[]{:S(2)}) collective-permute-start(bf16[256,4096]{1,0:T(8,128)(2,1)} %get-tuple-element.136), channel_id=1, source_target_pairs={{0,8},{1,9},{2,10},{3,11},{4,12},{5,13},{6,14},{7,15},{8,0},{9,1},... | collective-permute-start | bytes 6291464 | tf_op jit(solution)/shard_map/ppermute | solution.py:470
  87.1 22.4 %collective-permute-start.22 = (bf16[512,1024]{1,0:T(8,128)(2,1)}, bf16[512,1024]{1,0:T(8,128)(2,1)S(1)}, u32[]{:S(2)}, u32[]{:S(2)}) collective-permute-start(bf16[512,1024]{1,0:T(8,128)(2,1)} %get-tuple-element.116), channel_id=1, source_target_pairs={{0,8},{1,9},{2,10},{3,11},{4,12},{5,13},{6,14},{7,15},{8,0},{9,1},... | collective-permute-start | bytes 3145736 | tf_op jit(solution)/shard_map/ppermute | solution.py:470
  87.6 4.0 %collective-permute-start.5 = (bf16[144,512]{1,0:T(8,128)(2,1)}, bf16[144,512]{1,0:T(8,128)(2,1)S(1)}, u32[]{:S(2)}, u32[]{:S(2)}) collective-permute-start(bf16[144,512]{1,0:T(8,128)(2,1)} %get-tuple-element.88), channel_id=1, source_target_pairs={{0,120},{1,121},{2,122},{3,123},{4,124},{5,125},{6,126},{7,127},{8... | collective-permute-start | bytes 442376 | tf_op jit(solution)/shard_map/ppermute | solution.py:494
  108.3 17.9 %copy-start.51 = (bf16[144,512]{1,0:T(8,128)(2,1)S(1)}, bf16[144,512]{1,0:T(8,128)(2,1)}, u32[]{:S(2)}) copy-start(bf16[144,512]{1,0:T(8,128)(2,1)} %get-tuple-element.94) | copy-start | bytes 442372
  108.3 17.9 %collective-permute-start.7 = (bf16[256,2048]{1,0:T(8,128)(2,1)}, bf16[256,2048]{1,0:T(8,128)(2,1)S(1)}, u32[]{:S(2)}, u32[]{:S(2)}) collective-permute-start(bf16[256,2048]{1,0:T(8,128)(2,1)} %get-tuple-element.96), channel_id=1, source_target_pairs={{0,8},{1,9},{2,10},{3,11},{4,12},{5,13},{6,14},{7,15},{8,0},{9,1},... | collective-permute-start | bytes 3145736 | tf_op jit(solution)/shard_map/ppermute | solution.py:470
  113.1 7.9 %collective-permute-start.23 = (bf16[4,32,512]{2,1,0:T(8,128)(2,1)}, bf16[4,32,512]{2,1,0:T(8,128)(2,1)S(1)}, u32[]{:S(2)}, u32[]{:S(2)}) collective-permute-start(bf16[4,32,512]{2,1,0:T(8,128)(2,1)} %get-tuple-element.118), channel_id=1, source_target_pairs={{0,2},{1,3},{2,4},{3,5},{4,6},{5,7},{6,0},{7,1},{8,10},{9,11},{10,... | collective-permute-start | bytes 393224 | tf_op jit(solution)/shard_map/ppermute | solution.py:474
  115.0 10.0 %collective-permute-start.24 = (bf16[4,32,512]{2,1,0:T(8,128)(2,1)}, bf16[4,32,512]{2,1,0:T(8,128)(2,1)S(1)}, u32[]{:S(2)}, u32[]{:S(2)}) collective-permute-start(bf16[4,32,512]{2,1,0:T(8,128)(2,1)} %get-tuple-element.119), channel_id=1, source_target_pairs={{0,4},{1,5},{2,6},{3,7},{4,0},{5,1},{6,2},{7,3},{8,12},{9,13},{10,... | collective-permute-start | bytes 393224 | tf_op jit(solution)/shard_map/ppermute | solution.py:474
  118.6 7.1 %collective-permute-start.25 = (bf16[4,32,512]{2,1,0:T(8,128)(2,1)}, bf16[4,32,512]{2,1,0:T(8,128)(2,1)S(1)}, u32[]{:S(2)}, u32[]{:S(2)}) collective-permute-start(bf16[4,32,512]{2,1,0:T(8,128)(2,1)} %get-tuple-element.120), channel_id=1, source_target_pairs={{0,6},{1,7},{2,0},{3,1},{4,2},{5,3},{6,4},{7,5},{8,14},{9,15},{10,... | collective-permute-start | bytes 393224 | tf_op jit(solution)/shard_map/ppermute | solution.py:474
  121.0 8.8 %collective-permute-start.26 = (bf16[4,32,512]{2,1,0:T(8,128)(2,1)}, bf16[4,32,512]{2,1,0:T(8,128)(2,1)S(1)}, u32[]{:S(2)}, u32[]{:S(2)}) collective-permute-start(bf16[4,32,512]{2,1,0:T(8,128)(2,1)} %get-tuple-element.122), channel_id=1, source_target_pairs={{0,32},{1,33},{2,34},{3,35},{4,36},{5,37},{6,38},{7,39},{8,40},{9,... | collective-permute-start | bytes 393224 | tf_op jit(solution)/shard_map/ppermute | solution.py:478
  125.0 7.0 %collective-permute-start.27 = (bf16[4,32,512]{2,1,0:T(8,128)(2,1)}, bf16[4,32,512]{2,1,0:T(8,128)(2,1)S(1)}, u32[]{:S(2)}, u32[]{:S(2)}) collective-permute-start(bf16[4,32,512]{2,1,0:T(8,128)(2,1)} %get-tuple-element.123), channel_id=1, source_target_pairs={{0,64},{1,65},{2,66},{3,67},{4,68},{5,69},{6,70},{7,71},{8,72},{9,... | collective-permute-start | bytes 393224 | tf_op jit(solution)/shard_map/ppermute | solution.py:478
  125.7 8.2 %collective-permute-start.28 = (bf16[4,32,512]{2,1,0:T(8,128)(2,1)}, bf16[4,32,512]{2,1,0:T(8,128)(2,1)S(1)}, u32[]{:S(2)}, u32[]{:S(2)}) collective-permute-start(bf16[4,32,512]{2,1,0:T(8,128)(2,1)} %get-tuple-element.124), channel_id=1, source_target_pairs={{0,96},{1,97},{2,98},{3,99},{4,100},{5,101},{6,102},{7,103},{8,104... | collective-permute-start | bytes 393224 | tf_op jit(solution)/shard_map/ppermute | solution.py:478
  126.2 17.1 %collective-permute-start.6 = (bf16[144,512]{1,0:T(8,128)(2,1)S(1)}, bf16[144,512]{1,0:T(8,128)(2,1)S(1)}, u32[]{:S(2)}, u32[]{:S(2)}) collective-permute-start(bf16[144,512]{1,0:T(8,128)(2,1)S(1)} %copy-done.51), channel_id=1, source_target_pairs={{0,8},{1,9},{2,10},{3,11},{4,12},{5,13},{6,14},{7,15},{8,16},{9,17... | collective-permute-start | bytes 442376 | tf_op jit(solution)/shard_map/ppermute | solution.py:494
  129.8 16.3 %collective-permute-start.8 = (bf16[4,16,1024]{2,1,0:T(8,128)(2,1)}, bf16[4,16,1024]{2,1,0:T(8,128)(2,1)S(1)}, u32[]{:S(2)}, u32[]{:S(2)}) collective-permute-start(bf16[4,16,1024]{2,1,0:T(8,128)(2,1)} %get-tuple-element.98), channel_id=1, source_target_pairs={{0,2},{1,3},{2,4},{3,5},{4,6},{5,7},{6,0},{7,1},{8,10},{9,11},{10,... | collective-permute-start | bytes 393224 | tf_op jit(solution)/shard_map/ppermute | solution.py:474
  132.0 17.9 %collective-permute-start.9 = (bf16[4,16,1024]{2,1,0:T(8,128)(2,1)}, bf16[4,16,1024]{2,1,0:T(8,128)(2,1)S(1)}, u32[]{:S(2)}, u32[]{:S(2)}) collective-permute-start(bf16[4,16,1024]{2,1,0:T(8,128)(2,1)} %get-tuple-element.99), channel_id=1, source_target_pairs={{0,4},{1,5},{2,6},{3,7},{4,0},{5,1},{6,2},{7,3},{8,12},{9,13},{10,... | collective-permute-start | bytes 393224 | tf_op jit(solution)/shard_map/ppermute | solution.py:474
  136.6 8.8 %collective-permute-start.29 = (bf16[32,512]{1,0:T(8,128)(2,1)}, bf16[32,512]{1,0:T(8,128)(2,1)S(1)}, u32[]{:S(2)}, u32[]{:S(2)}) collective-permute-start(bf16[32,512]{1,0:T(8,128)(2,1)} %get-tuple-element.126), channel_id=1, source_target_pairs={{0,32},{1,33},{2,34},{3,35},{4,36},{5,37},{6,38},{7,39},{8,40},{9,... | collective-permute-start | bytes 98312 | tf_op jit(solution)/shard_map/ppermute | solution.py:478
  138.3 17.8 %copy-start.58 = (bf16[32,512]{1,0:T(8,128)(2,1)S(1)}, bf16[32,512]{1,0:T(8,128)(2,1)}, u32[]{:S(2)}) copy-start(bf16[32,512]{1,0:T(8,128)(2,1)} %get-tuple-element.130) | copy-start | bytes 98308
  138.3 18.0 %copy-start.57 = (bf16[32,512]{1,0:T(8,128)(2,1)S(1)}, bf16[32,512]{1,0:T(8,128)(2,1)}, u32[]{:S(2)}) copy-start(bf16[32,512]{1,0:T(8,128)(2,1)} %get-tuple-element.131) | copy-start | bytes 98308
  138.4 21.9 %copy-start.56 = (bf16[32,512]{1,0:T(8,128)(2,1)S(1)}, bf16[32,512]{1,0:T(8,128)(2,1)}, u32[]{:S(2)}) copy-start(bf16[32,512]{1,0:T(8,128)(2,1)} %get-tuple-element.132) | copy-start | bytes 98308
  138.4 43.4 %copy-start.6 = (bf16[144,1024]{1,0:T(8,128)(2,1)S(1)}, bf16[144,1024]{1,0:T(8,128)(2,1)}, u32[]{:S(2)}) copy-start(bf16[144,1024]{1,0:T(8,128)(2,1)} %get-tuple-element.83) | copy-start | bytes 884740
  142.1 35.4 %collective-permute-start.37 = (bf16[4,16,2048]{2,1,0:T(8,128)(2,1)}, bf16[4,16,2048]{2,1,0:T(8,128)(2,1)S(1)}, u32[]{:S(2)}, u32[]{:S(2)}) collective-permute-start(bf16[4,16,2048]{2,1,0:T(8,128)(2,1)} %get-tuple-element.138), channel_id=1, source_target_pairs={{0,2},{1,3},{2,4},{3,5},{4,6},{5,7},{6,0},{7,1},{8,10},{9,11},{10,... | collective-permute-start | bytes 786440 | tf_op jit(solution)/shard_map/ppermute | solution.py:474
  143.3 39.7 %copy-start.17 = (bf16[144,512]{1,0:T(8,128)(2,1)}, bf16[144,512]{1,0:T(8,128)(2,1)S(1)}, u32[]{:S(2)}) copy-start(bf16[144,512]{1,0:T(8,128)(2,1)S(1)} %collective-permute-done.6.tail) | copy-start | bytes 442372
  143.3 6.8 %collective-permute-start.10 = (bf16[4,16,1024]{2,1,0:T(8,128)(2,1)S(1)}, bf16[4,16,1024]{2,1,0:T(8,128)(2,1)S(1)}, u32[]{:S(2)}, u32[]{:S(2)}) collective-permute-start(bf16[4,16,1024]{2,1,0:T(8,128)(2,1)S(1)} %copy-done.55), channel_id=1, source_target_pairs={{0,6},{1,7},{2,0},{3,1},{4,2},{5,3},{6,4},{7,5},{8,14},{9,15},{10,... | collective-permute-start | bytes 393224 | tf_op jit(solution)/shard_map/ppermute | solution.py:474
  145.4 40.4 %copy-start.39 = (bf16[32,512]{1,0:T(8,128)(2,1)}, bf16[32,512]{1,0:T(8,128)(2,1)S(1)}, u32[]{:S(2)}) copy-start(bf16[32,512]{1,0:T(8,128)(2,1)S(1)} %collective-permute-done.29.refs_1_) | copy-start | bytes 98308
  145.4 6.5 %collective-permute-start.11 = (bf16[4,16,1024]{2,1,0:T(8,128)(2,1)S(1)}, bf16[4,16,1024]{2,1,0:T(8,128)(2,1)S(1)}, u32[]{:S(2)}, u32[]{:S(2)}) collective-permute-start(bf16[4,16,1024]{2,1,0:T(8,128)(2,1)S(1)} %copy-done.54), channel_id=1, source_target_pairs={{0,32},{1,33},{2,34},{3,35},{4,36},{5,37},{6,38},{7,39},{8,40},{9,... | collective-permute-start | bytes 393224 | tf_op jit(solution)/shard_map/ppermute | solution.py:478
  146.1 10.0 %collective-permute-start.12 = (bf16[4,16,1024]{2,1,0:T(8,128)(2,1)S(1)}, bf16[4,16,1024]{2,1,0:T(8,128)(2,1)S(1)}, u32[]{:S(2)}, u32[]{:S(2)}) collective-permute-start(bf16[4,16,1024]{2,1,0:T(8,128)(2,1)S(1)} %copy-done.53), channel_id=1, source_target_pairs={{0,64},{1,65},{2,66},{3,67},{4,68},{5,69},{6,70},{7,71},{8,72},{9,... | collective-permute-start | bytes 393224 | tf_op jit(solution)/shard_map/ppermute | solution.py:478
  149.9 6.5 %collective-permute-start.13 = (bf16[4,16,1024]{2,1,0:T(8,128)(2,1)S(1)}, bf16[4,16,1024]{2,1,0:T(8,128)(2,1)S(1)}, u32[]{:S(2)}, u32[]{:S(2)}) collective-permute-start(bf16[4,16,1024]{2,1,0:T(8,128)(2,1)S(1)} %copy-done.52), channel_id=1, source_target_pairs={{0,96},{1,97},{2,98},{3,99},{4,100},{5,101},{6,102},{7,103},{8,104... | collective-permute-start | bytes 393224 | tf_op jit(solution)/shard_map/ppermute | solution.py:478
  150.2 10.1 %collective-permute-start.30 = (bf16[32,512]{1,0:T(8,128)(2,1)S(1)}, bf16[32,512]{1,0:T(8,128)(2,1)S(1)}, u32[]{:S(2)}, u32[]{:S(2)}) collective-permute-start(bf16[32,512]{1,0:T(8,128)(2,1)S(1)} %copy-done.60), channel_id=1, source_target_pairs={{0,64},{1,65},{2,66},{3,67},{4,68},{5,69},{6,70},{7,71},{8,72},{9,... | collective-permute-start | bytes 98312 | tf_op jit(solution)/shard_map/ppermute | solution.py:478
  151.9 10.5 %collective-permute-start.31 = (bf16[32,512]{1,0:T(8,128)(2,1)S(1)}, bf16[32,512]{1,0:T(8,128)(2,1)S(1)}, u32[]{:S(2)}, u32[]{:S(2)}) collective-permute-start(bf16[32,512]{1,0:T(8,128)(2,1)S(1)} %copy-done.59), channel_id=1, source_target_pairs={{0,96},{1,97},{2,98},{3,99},{4,100},{5,101},{6,102},{7,103},{8,104... | collective-permute-start | bytes 98312 | tf_op jit(solution)/shard_map/ppermute | solution.py:478
  156.1 6.3 %collective-permute-start.32 = (bf16[32,512]{1,0:T(8,128)(2,1)S(1)}, bf16[32,512]{1,0:T(8,128)(2,1)S(1)}, u32[]{:S(2)}, u32[]{:S(2)}) collective-permute-start(bf16[32,512]{1,0:T(8,128)(2,1)S(1)} %copy-done.58), channel_id=1, source_target_pairs={{0,2},{1,3},{2,4},{3,5},{4,6},{5,7},{6,0},{7,1},{8,10},{9,11},{10,... | collective-permute-start | bytes 98312 | tf_op jit(solution)/shard_map/ppermute | solution.py:474
  156.4 8.5 %collective-permute-start.33 = (bf16[32,512]{1,0:T(8,128)(2,1)S(1)}, bf16[32,512]{1,0:T(8,128)(2,1)S(1)}, u32[]{:S(2)}, u32[]{:S(2)}) collective-permute-start(bf16[32,512]{1,0:T(8,128)(2,1)S(1)} %copy-done.57), channel_id=1, source_target_pairs={{0,4},{1,5},{2,6},{3,7},{4,0},{5,1},{6,2},{7,3},{8,12},{9,13},{10,... | collective-permute-start | bytes 98312 | tf_op jit(solution)/shard_map/ppermute | solution.py:474
  160.3 25.5 %copy-start.40 = (bf16[32,512]{1,0:T(8,128)(2,1)}, bf16[32,512]{1,0:T(8,128)(2,1)S(1)}, u32[]{:S(2)}) copy-start(bf16[32,512]{1,0:T(8,128)(2,1)S(1)} %collective-permute-done.30.refs_2_) | copy-start | bytes 98308
  160.3 5.5 %collective-permute-start.34 = (bf16[32,512]{1,0:T(8,128)(2,1)S(1)}, bf16[32,512]{1,0:T(8,128)(2,1)S(1)}, u32[]{:S(2)}, u32[]{:S(2)}) collective-permute-start(bf16[32,512]{1,0:T(8,128)(2,1)S(1)} %copy-done.56), channel_id=1, source_target_pairs={{0,6},{1,7},{2,0},{3,1},{4,2},{5,3},{6,4},{7,5},{8,14},{9,15},{10,... | collective-permute-start | bytes 98312 | tf_op jit(solution)/shard_map/ppermute | solution.py:474
  162.3 23.4 %copy-start.41 = (bf16[32,512]{1,0:T(8,128)(2,1)}, bf16[32,512]{1,0:T(8,128)(2,1)S(1)}, u32[]{:S(2)}) copy-start(bf16[32,512]{1,0:T(8,128)(2,1)S(1)} %collective-permute-done.31.refs_3_) | copy-start | bytes 98308
  162.3 5.3 %collective-permute-start.14 = (bf16[16,1024]{1,0:T(8,128)(2,1)}, bf16[16,1024]{1,0:T(8,128)(2,1)S(1)}, u32[]{:S(2)}, u32[]{:S(2)}) collective-permute-start(bf16[16,1024]{1,0:T(8,128)(2,1)} %get-tuple-element.106), channel_id=1, source_target_pairs={{0,32},{1,33},{2,34},{3,35},{4,36},{5,37},{6,38},{7,39},{8,40},{9,... | collective-permute-start | bytes 98312 | tf_op jit(solution)/shard_map/ppermute | solution.py:478
  162.5 23.3 %copy-start.42 = (bf16[32,512]{1,0:T(8,128)(2,1)}, bf16[32,512]{1,0:T(8,128)(2,1)S(1)}, u32[]{:S(2)}) copy-start(bf16[32,512]{1,0:T(8,128)(2,1)S(1)} %collective-permute-done.32.refs_5_) | copy-start | bytes 98308
  162.5 7.6 %collective-permute-start.15 = (bf16[16,1024]{1,0:T(8,128)(2,1)}, bf16[16,1024]{1,0:T(8,128)(2,1)S(1)}, u32[]{:S(2)}, u32[]{:S(2)}) collective-permute-start(bf16[16,1024]{1,0:T(8,128)(2,1)} %get-tuple-element.107), channel_id=1, source_target_pairs={{0,64},{1,65},{2,66},{3,67},{4,68},{5,69},{6,70},{7,71},{8,72},{9,... | collective-permute-start | bytes 98312 | tf_op jit(solution)/shard_map/ppermute | solution.py:478
  164.9 20.9 %copy-start.43 = (bf16[32,512]{1,0:T(8,128)(2,1)}, bf16[32,512]{1,0:T(8,128)(2,1)S(1)}, u32[]{:S(2)}) copy-start(bf16[32,512]{1,0:T(8,128)(2,1)S(1)} %collective-permute-done.33.refs_6_) | copy-start | bytes 98308
  164.9 5.9 %collective-permute-start.16 = (bf16[16,1024]{1,0:T(8,128)(2,1)}, bf16[16,1024]{1,0:T(8,128)(2,1)S(1)}, u32[]{:S(2)}, u32[]{:S(2)}) collective-permute-start(bf16[16,1024]{1,0:T(8,128)(2,1)} %get-tuple-element.108), channel_id=1, source_target_pairs={{0,96},{1,97},{2,98},{3,99},{4,100},{5,101},{6,102},{7,103},{8,104... | collective-permute-start | bytes 98312 | tf_op jit(solution)/shard_map/ppermute | solution.py:478
  165.8 20.1 %copy-start.44 = (bf16[32,512]{1,0:T(8,128)(2,1)}, bf16[32,512]{1,0:T(8,128)(2,1)S(1)}, u32[]{:S(2)}) copy-start(bf16[32,512]{1,0:T(8,128)(2,1)S(1)} %collective-permute-done.34.refs_7_) | copy-start | bytes 98308
  165.8 6.2 %collective-permute-start.17 = (bf16[16,1024]{1,0:T(8,128)(2,1)}, bf16[16,1024]{1,0:T(8,128)(2,1)S(1)}, u32[]{:S(2)}, u32[]{:S(2)}) collective-permute-start(bf16[16,1024]{1,0:T(8,128)(2,1)} %get-tuple-element.110), channel_id=1, source_target_pairs={{0,2},{1,3},{2,4},{3,5},{4,6},{5,7},{6,0},{7,1},{8,10},{9,11},{10,... | collective-permute-start | bytes 98312 | tf_op jit(solution)/shard_map/ppermute | solution.py:474
  167.7 7.1 %collective-permute-start.18 = (bf16[16,1024]{1,0:T(8,128)(2,1)}, bf16[16,1024]{1,0:T(8,128)(2,1)S(1)}, u32[]{:S(2)}, u32[]{:S(2)}) collective-permute-start(bf16[16,1024]{1,0:T(8,128)(2,1)} %get-tuple-element.111), channel_id=1, source_target_pairs={{0,4},{1,5},{2,6},{3,7},{4,0},{5,1},{6,2},{7,3},{8,12},{9,13},{10,... | collective-permute-start | bytes 98312 | tf_op jit(solution)/shard_map/ppermute | solution.py:474
  170.1 4.7 %collective-permute-start.19 = (bf16[16,1024]{1,0:T(8,128)(2,1)}, bf16[16,1024]{1,0:T(8,128)(2,1)S(1)}, u32[]{:S(2)}, u32[]{:S(2)}) collective-permute-start(bf16[16,1024]{1,0:T(8,128)(2,1)} %get-tuple-element.112), channel_id=1, source_target_pairs={{0,6},{1,7},{2,0},{3,1},{4,2},{5,3},{6,4},{7,5},{8,14},{9,15},{10,... | collective-permute-start | bytes 98312 | tf_op jit(solution)/shard_map/ppermute | solution.py:474
  170.8 9.2 %collective-permute-start.38 = (bf16[4,16,2048]{2,1,0:T(8,128)(2,1)}, bf16[4,16,2048]{2,1,0:T(8,128)(2,1)S(1)}, u32[]{:S(2)}, u32[]{:S(2)}) collective-permute-start(bf16[4,16,2048]{2,1,0:T(8,128)(2,1)} %get-tuple-element.139), channel_id=1, source_target_pairs={{0,4},{1,5},{2,6},{3,7},{4,0},{5,1},{6,2},{7,3},{8,12},{9,13},{10,... | collective-permute-start | bytes 786440 | tf_op jit(solution)/shard_map/ppermute | solution.py:474
  171.9 15.4 %collective-permute-start.39 = (bf16[4,16,2048]{2,1,0:T(8,128)(2,1)}, bf16[4,16,2048]{2,1,0:T(8,128)(2,1)S(1)}, u32[]{:S(2)}, u32[]{:S(2)}) collective-permute-start(bf16[4,16,2048]{2,1,0:T(8,128)(2,1)} %get-tuple-element.140), channel_id=1, source_target_pairs={{0,6},{1,7},{2,0},{3,1},{4,2},{5,3},{6,4},{7,5},{8,14},{9,15},{10,... | collective-permute-start | bytes 786440 | tf_op jit(solution)/shard_map/ppermute | solution.py:474
  174.8 12.9 %collective-permute-start.40 = (bf16[4,16,2048]{2,1,0:T(8,128)(2,1)}, bf16[4,16,2048]{2,1,0:T(8,128)(2,1)S(1)}, u32[]{:S(2)}, u32[]{:S(2)}) collective-permute-start(bf16[4,16,2048]{2,1,0:T(8,128)(2,1)} %get-tuple-element.142), channel_id=1, source_target_pairs={{0,32},{1,33},{2,34},{3,35},{4,36},{5,37},{6,38},{7,39},{8,40},{9,... | collective-permute-start | bytes 786440 | tf_op jit(solution)/shard_map/ppermute | solution.py:478
  174.8 12.9 %collective-permute-start.41 = (bf16[4,16,2048]{2,1,0:T(8,128)(2,1)}, bf16[4,16,2048]{2,1,0:T(8,128)(2,1)S(1)}, u32[]{:S(2)}, u32[]{:S(2)}) collective-permute-start(bf16[4,16,2048]{2,1,0:T(8,128)(2,1)} %get-tuple-element.143), channel_id=1, source_target_pairs={{0,64},{1,65},{2,66},{3,67},{4,68},{5,69},{6,70},{7,71},{8,72},{9,... | collective-permute-start | bytes 786440 | tf_op jit(solution)/shard_map/ppermute | solution.py:478
  177.5 10.2 %collective-permute-start.42 = (bf16[4,16,2048]{2,1,0:T(8,128)(2,1)}, bf16[4,16,2048]{2,1,0:T(8,128)(2,1)S(1)}, u32[]{:S(2)}, u32[]{:S(2)}) collective-permute-start(bf16[4,16,2048]{2,1,0:T(8,128)(2,1)} %get-tuple-element.144), channel_id=1, source_target_pairs={{0,96},{1,97},{2,98},{3,99},{4,100},{5,101},{6,102},{7,103},{8,104... | collective-permute-start | bytes 786440 | tf_op jit(solution)/shard_map/ppermute | solution.py:478
  180.0 13.7 %collective-permute-start.20 = (bf16[8,2048]{1,0:T(8,128)(2,1)}, bf16[8,2048]{1,0:T(8,128)(2,1)S(1)}, u32[]{:S(2)}, u32[]{:S(2)}) collective-permute-start(bf16[8,2048]{1,0:T(8,128)(2,1)} %get-tuple-element.114), channel_id=1, source_target_pairs={{0,16},{1,17},{2,18},{3,19},{4,20},{5,21},{6,22},{7,23},{8,24},{9,... | collective-permute-start | bytes 98312 | tf_op jit(solution)/shard_map/ppermute | solution.py:482
  187.3 11.3 %collective-permute-start.35 = (bf16[16,1024]{1,0:T(8,128)(2,1)}, bf16[16,1024]{1,0:T(8,128)(2,1)S(1)}, u32[]{:S(2)}, u32[]{:S(2)}) collective-permute-start(bf16[16,1024]{1,0:T(8,128)(2,1)} %get-tuple-element.134), channel_id=1, source_target_pairs={{0,16},{1,17},{2,18},{3,19},{4,20},{5,21},{6,22},{7,23},{8,24},{9,... | collective-permute-start | bytes 98312 | tf_op jit(solution)/shard_map/ppermute | solution.py:482
  191.0 8.8 %collective-permute-start.43 = (bf16[16,2048]{1,0:T(8,128)(2,1)}, bf16[16,2048]{1,0:T(8,128)(2,1)S(1)}, u32[]{:S(2)}, u32[]{:S(2)}) collective-permute-start(bf16[16,2048]{1,0:T(8,128)(2,1)} %get-tuple-element.146), channel_id=1, source_target_pairs={{0,32},{1,33},{2,34},{3,35},{4,36},{5,37},{6,38},{7,39},{8,40},{9,... | collective-permute-start | bytes 196616 | tf_op jit(solution)/shard_map/ppermute | solution.py:478
  192.1 9.0 %collective-permute-start.44 = (bf16[16,2048]{1,0:T(8,128)(2,1)}, bf16[16,2048]{1,0:T(8,128)(2,1)S(1)}, u32[]{:S(2)}, u32[]{:S(2)}) collective-permute-start(bf16[16,2048]{1,0:T(8,128)(2,1)} %get-tuple-element.147), channel_id=1, source_target_pairs={{0,64},{1,65},{2,66},{3,67},{4,68},{5,69},{6,70},{7,71},{8,72},{9,... | collective-permute-start | bytes 196616 | tf_op jit(solution)/shard_map/ppermute | solution.py:478
  193.7 15.3 %collective-permute-start.21 = (bf16[4,2048]{1,0:T(4,128)(2,1)S(1)}, bf16[4,2048]{1,0:T(4,128)(2,1)S(1)}, u32[]{:S(2)}, u32[]{:S(2)}) collective-permute-start(bf16[4,2048]{1,0:T(4,128)(2,1)S(1)} %slice.40), channel_id=1, source_target_pairs={{0,1},{1,0},{2,3},{3,2},{4,5},{5,4},{6,7},{7,6},{8,9},{9,8},{10,11... | collective-permute-start | bytes 49160 | tf_op jit(solution)/shard_map/ppermute | solution.py:486
  196.1 7.1 %collective-permute-start.45 = (bf16[16,2048]{1,0:T(8,128)(2,1)}, bf16[16,2048]{1,0:T(8,128)(2,1)S(1)}, u32[]{:S(2)}, u32[]{:S(2)}) collective-permute-start(bf16[16,2048]{1,0:T(8,128)(2,1)} %get-tuple-element.148), channel_id=1, source_target_pairs={{0,96},{1,97},{2,98},{3,99},{4,100},{5,101},{6,102},{7,103},{8,104... | collective-permute-start | bytes 196616 | tf_op jit(solution)/shard_map/ppermute | solution.py:478
  198.6 5.7 %collective-permute-start.46 = (bf16[16,2048]{1,0:T(8,128)(2,1)}, bf16[16,2048]{1,0:T(8,128)(2,1)S(1)}, u32[]{:S(2)}, u32[]{:S(2)}) collective-permute-start(bf16[16,2048]{1,0:T(8,128)(2,1)} %get-tuple-element.150), channel_id=1, source_target_pairs={{0,2},{1,3},{2,4},{3,5},{4,6},{5,7},{6,0},{7,1},{8,10},{9,11},{10,... | collective-permute-start | bytes 196616 | tf_op jit(solution)/shard_map/ppermute | solution.py:474
  199.7 6.0 %collective-permute-start.47 = (bf16[16,2048]{1,0:T(8,128)(2,1)}, bf16[16,2048]{1,0:T(8,128)(2,1)S(1)}, u32[]{:S(2)}, u32[]{:S(2)}) collective-permute-start(bf16[16,2048]{1,0:T(8,128)(2,1)} %get-tuple-element.151), channel_id=1, source_target_pairs={{0,4},{1,5},{2,6},{3,7},{4,0},{5,1},{6,2},{7,3},{8,12},{9,13},{10,... | collective-permute-start | bytes 196616 | tf_op jit(solution)/shard_map/ppermute | solution.py:474
  201.1 4.7 %collective-permute-start.48 = (bf16[16,2048]{1,0:T(8,128)(2,1)}, bf16[16,2048]{1,0:T(8,128)(2,1)S(1)}, u32[]{:S(2)}, u32[]{:S(2)}) collective-permute-start(bf16[16,2048]{1,0:T(8,128)(2,1)} %get-tuple-element.152), channel_id=1, source_target_pairs={{0,6},{1,7},{2,0},{3,1},{4,2},{5,3},{6,4},{7,5},{8,14},{9,15},{10,... | collective-permute-start | bytes 196616 | tf_op jit(solution)/shard_map/ppermute | solution.py:474
  208.2 4.5 %collective-permute-start.49 = (bf16[8,4096]{1,0:T(8,128)(2,1)}, bf16[8,4096]{1,0:T(8,128)(2,1)S(1)}, u32[]{:S(2)}, u32[]{:S(2)}) collective-permute-start(bf16[8,4096]{1,0:T(8,128)(2,1)} %get-tuple-element.154), channel_id=1, source_target_pairs={{0,16},{1,17},{2,18},{3,19},{4,20},{5,21},{6,22},{7,23},{8,24},{9,... | collective-permute-start | bytes 196616 | tf_op jit(solution)/shard_map/ppermute | solution.py:482
  (47 other events, 247.4 us)
